TPU v7x, 32 devices: a whole 2x2x4 slice. The times are simulated.
32 devices in a mesh: dp: 32 (over z, y, x, core).
Axes of the slice: x: 2, y: 2, z: 4, core: 2. Of those that a mesh axis runs over, the one named last changes fastest.
Arguments:
- images: bfloat16 [256, 197, 512], P('dp'), may hold values from -6 to 6
- image_count: int32 [32], P('dp'), may hold values from 1 to 8, as said below
- expert_index: int32 [256, 197, 2], P('dp'), may hold values from 0 to 7, as said below
- expert_slot: int32 [256, 197, 2], P('dp'), may hold values from 0 to 127, as said below
- keep: int32 [256, 197, 2], P('dp'), may hold values from 0 to 1, as said below
- cotangent: bfloat16 [256, 197, 512], P('dp'), may hold values from -6 to 6
- ln1_gain: bfloat16 [512], P('dp'), may hold values from 0.5 to 1.5
- ln1_bias: bfloat16 [512], P('dp'), may hold values from -1.1953125 to 1.1953125
- qkv_weight: bfloat16 [512, 1536], P('dp'), may hold values from -0.375 to 0.375
- qv_bias: bfloat16 [2, 512], P(None, 'dp'), may hold values from -1.796875 to 1.796875
- out_weight: bfloat16 [512, 512], P('dp'), may hold values from -0.75 to 0.75
- out_bias: bfloat16 [512], P('dp'), may hold values from -0.59765625 to 0.59765625
- ln2_gain: bfloat16 [512], P('dp'), may hold values from 0.5 to 1.5
- ln2_bias: bfloat16 [512], P('dp'), may hold values from -0.59765625 to 0.59765625
- router_weight: bfloat16 [512, 8], P('dp'), may hold values from -0.1875 to 0.1875
- expert_in: bfloat16 [8, 512, 2048], P(None, 'dp'), may hold values from -0.25 to 0.25
- expert_in_bias: bfloat16 [8, 2048], P(None, 'dp'), may hold values from -1.1953125 to 1.1953125
- expert_out: bfloat16 [8, 2048, 512], P(None, 'dp'), may hold values from -0.75 to 0.75
- expert_out_bias: bfloat16 [8, 512], P(None, 'dp'), may hold values from -2.3 to 2.3
Outputs:
- block_out: bfloat16 [256, 197, 512], P('dp')
- image_grad: bfloat16 [256, 197, 512], P('dp')
- balance: float32 [], replicated
- ln1_gain_grad: float32 [512], P('dp')
- ln1_bias_grad: float32 [512], P('dp')
- qkv_weight_grad: float32 [512, 1536], P('dp')
- qv_bias_grad: float32 [2, 512], P(None, 'dp')
- out_weight_grad: float32 [512, 512], P('dp')
- out_bias_grad: float32 [512], P('dp')
- ln2_gain_grad: float32 [512], P('dp')
- ln2_bias_grad: float32 [512], P('dp')
- router_weight_grad: float32 [512, 8], P('dp')
- expert_in_grad: float32 [8, 512, 2048], P(None, 'dp')
- expert_in_bias_grad: float32 [8, 2048], P(None, 'dp')
- expert_out_grad: float32 [8, 2048, 512], P(None, 'dp')
- expert_out_bias_grad: float32 [8, 512], P(None, 'dp')
Inputs may be any that keep to these rules, and one draw needn't show every extreme that they name: Device d's live images fill its first image_count[d] slots; some device has all 8 slots live. `expert_index`: the two experts of a token differ. `expert_slot`: within one micro-batch of one device, the dispatched choices of one expert have distinct positions; choices that are not dispatched hold 0. In some micro-batch some expert uses all 128 positions. `keep`: choices of tokens in padding slots are never dispatched.
All inputs are finite; a program needn't handle non-finite values.
Results may differ from a plain program's by a relative error of at most 0.014.
Values may be sent and summed in bfloat16 or wider, within the bound.
No kernel may reach another device: no remote copies, remote signals or barrier semaphores. Data moves between devices by JAX's collectives and lax.ppermute only.
A program may use at most 384 MiB of HBM per device.

v0:
```python
import jax
import jax.numpy as jnp
from jax import lax
from jax.sharding import PartitionSpec as P

HEADS = 8
HEAD_DIM = 64
EXPERTS = 8
MICRO = 4
CAP = 128


EPSILON = 1e-06
BALANCE_WEIGHT = 8.0


def layer_norm(values, gain_vec, shift_vec):
    average = jnp.mean(values, -1, keepdims=True)
    centered = values - average
    spread = jnp.mean(centered * centered, -1, keepdims=True)
    return centered * lax.rsqrt(spread + EPSILON) * gain_vec + shift_vec


def gelu_exact(pre_act):
    return jax.nn.gelu(pre_act, approximate=False)


def forward_pass(gathered, tokens_in, routes, slot_pos, kept_flag, live_tok):
    (
        gain_one,
        shift_one,
        qkv_mat,
        qv_vec,
        out_mat,
        out_vec,
        gain_two,
        shift_two,
        router_mat,
        inner_mat,
        inner_vec,
        outer_mat,
        outer_vec,
    ) = gathered
    image_rows = tokens_in.shape[0]
    seq_len = tokens_in.shape[1]
    model_width = tokens_in.shape[2]
    row_count = image_rows * seq_len
    expert_total = inner_mat.shape[0]
    scale_val = HEAD_DIM ** (-0.5)
    flat_tok = tokens_in.reshape(row_count, model_width).astype(jnp.float32)
    normed = layer_norm(
        flat_tok, gain_one.astype(jnp.float32), shift_one.astype(jnp.float32)
    ).astype(jnp.bfloat16)
    bias_full = jnp.concatenate(
        [
            qv_vec[0].astype(jnp.float32),
            jnp.zeros((model_width,), jnp.float32),
            qv_vec[1].astype(jnp.float32),
        ]
    )
    projected = (jnp.dot(normed, qkv_mat, preferred_element_type=jnp.float32) + bias_full).astype(
        jnp.bfloat16
    )
    head_shape = (image_rows, seq_len, HEADS, HEAD_DIM)
    query_part = projected[:, :model_width].reshape(head_shape)
    key_part = projected[:, model_width : 2 * model_width].reshape(head_shape)
    value_part = projected[:, 2 * model_width :].reshape(head_shape)
    scores = (
        jnp.einsum("bqhd,bkhd->bhqk", query_part, key_part, preferred_element_type=jnp.float32)
        * scale_val
    )
    attn_prob = jax.nn.softmax(scores, axis=-1)
    prob_low = attn_prob.astype(jnp.bfloat16)
    attended = (
        jnp.einsum("bhqk,bkhd->bqhd", prob_low, value_part, preferred_element_type=jnp.float32)
        .astype(jnp.bfloat16)
        .reshape(row_count, model_width)
    )
    middle = (
        flat_tok
        + jnp.dot(attended, out_mat, preferred_element_type=jnp.float32)
        + out_vec.astype(jnp.float32)
    )
    mixed_in = layer_norm(
        middle, gain_two.astype(jnp.float32), shift_two.astype(jnp.float32)
    ).astype(jnp.bfloat16)
    logits = jnp.dot(mixed_in, router_mat, preferred_element_type=jnp.float32)
    router_prob = jax.nn.softmax(logits, axis=-1)
    target = jnp.where(kept_flag == 1, routes * CAP + slot_pos, expert_total * CAP)
    buffer = jnp.zeros((expert_total * CAP + 1, model_width), jnp.bfloat16)
    buffer = buffer.at[target.reshape(-1)].set(jnp.repeat(mixed_in, 2, axis=0))
    expert_rows = buffer[: expert_total * CAP].reshape(expert_total, CAP, model_width)
    hidden_pre = (
        jnp.einsum("ecd,edf->ecf", expert_rows, inner_mat, preferred_element_type=jnp.float32)
        + inner_vec.astype(jnp.float32)[:, None, :]
    )
    activated = gelu_exact(hidden_pre).astype(jnp.bfloat16)
    expert_res = (
        jnp.einsum("ecf,efd->ecd", activated, outer_mat, preferred_element_type=jnp.float32)
        + outer_vec.astype(jnp.float32)[:, None, :]
    )
    padded_res = jnp.concatenate(
        [
            expert_res.reshape(expert_total * CAP, model_width),
            jnp.zeros((1, model_width), jnp.float32),
        ],
        0,
    )
    picked = padded_res[target]
    gate_vals = jnp.take_along_axis(router_prob, routes, axis=1) * kept_flag.astype(jnp.float32)
    final_sum = middle + jnp.sum(gate_vals[:, :, None] * picked, axis=1)
    result = final_sum * live_tok[:, None]
    return {
        "flat_tok": flat_tok,
        "normed": normed,
        "query_part": query_part,
        "key_part": key_part,
        "value_part": value_part,
        "attn_prob": attn_prob,
        "prob_low": prob_low,
        "attended": attended,
        "middle": middle,
        "mixed_in": mixed_in,
        "router_prob": router_prob,
        "target": target,
        "expert_rows": expert_rows,
        "hidden_pre": hidden_pre,
        "activated": activated,
        "picked": picked,
        "gate_vals": gate_vals,
        "result": result,
    }


def backward_pass(gathered, saved, cot_rows, live_tok, routes, kept_flag, balance_coef, grad_list):
    (
        gain_one,
        shift_one,
        qkv_mat,
        qv_vec,
        out_mat,
        out_vec,
        gain_two,
        shift_two,
        router_mat,
        inner_mat,
        inner_vec,
        outer_mat,
        outer_vec,
    ) = gathered
    flat_tok = saved["flat_tok"]
    row_count = flat_tok.shape[0]
    model_width = flat_tok.shape[1]
    expert_total = inner_mat.shape[0]
    image_rows = saved["query_part"].shape[0]
    seq_len = saved["query_part"].shape[1]
    scale_val = HEAD_DIM ** (-0.5)
    d_final = cot_rows.reshape(row_count, model_width).astype(jnp.float32) * live_tok[:, None]
    d_picked = saved["gate_vals"][:, :, None] * d_final[:, None, :]
    d_gates = jnp.sum(saved["picked"] * d_final[:, None, :], -1) * kept_flag.astype(jnp.float32)
    target = saved["target"]
    d_res = jnp.zeros((expert_total * CAP + 1, model_width), jnp.float32)
    d_res = d_res.at[target.reshape(-1)].add(d_picked.reshape(-1, model_width))
    d_res_low = (
        d_res[: expert_total * CAP].reshape(expert_total, CAP, model_width).astype(jnp.bfloat16)
    )
    grad_outer_vec = grad_list[12] + jnp.sum(d_res_low.astype(jnp.float32), 1)
    grad_outer = grad_list[11] + jnp.einsum(
        "ecf,ecd->efd", saved["activated"], d_res_low, preferred_element_type=jnp.float32
    )
    d_act = jnp.einsum("ecd,efd->ecf", d_res_low, outer_mat, preferred_element_type=jnp.float32)
    gelu_value, gelu_pull = jax.vjp(gelu_exact, saved["hidden_pre"])
    d_hidden = gelu_pull(d_act)[0].astype(jnp.bfloat16)
    grad_inner_vec = grad_list[10] + jnp.sum(d_hidden.astype(jnp.float32), 1)
    grad_inner = grad_list[9] + jnp.einsum(
        "ecd,ecf->edf", saved["expert_rows"], d_hidden, preferred_element_type=jnp.float32
    )
    d_rows = jnp.einsum("ecf,edf->ecd", d_hidden, inner_mat, preferred_element_type=jnp.float32)
    padded_rows = jnp.concatenate(
        [d_rows.reshape(expert_total * CAP, model_width), jnp.zeros((1, model_width), jnp.float32)],
        0,
    )
    d_mixed = jnp.sum(padded_rows[target], axis=1)
    route_hot = (routes[:, :, None] == jnp.arange(expert_total)[None, None, :]).astype(jnp.float32)
    d_prob = jnp.sum(route_hot * d_gates[:, :, None], 1) + balance_coef[None, :] * live_tok[:, None]
    router_prob = saved["router_prob"]
    d_logits = router_prob * (d_prob - jnp.sum(router_prob * d_prob, -1, keepdims=True))
    d_logit_low = d_logits.astype(jnp.bfloat16)
    grad_router = grad_list[8] + jnp.einsum(
        "td,te->de", saved["mixed_in"], d_logit_low, preferred_element_type=jnp.float32
    )
    d_mixed = d_mixed + jnp.einsum(
        "te,de->td", d_logit_low, router_mat, preferred_element_type=jnp.float32
    )
    norm_value, norm_pull = jax.vjp(
        layer_norm, saved["middle"], gain_two.astype(jnp.float32), shift_two.astype(jnp.float32)
    )
    d_mid_norm, d_gain_two, d_shift_two = norm_pull(d_mixed)
    d_middle = d_final + d_mid_norm
    grad_out_vec = grad_list[5] + jnp.sum(d_middle, 0)
    d_branch = d_middle.astype(jnp.bfloat16)
    grad_out = grad_list[4] + jnp.einsum(
        "td,te->de", saved["attended"], d_branch, preferred_element_type=jnp.float32
    )
    head_shape = (image_rows, seq_len, HEADS, HEAD_DIM)
    d_att = (
        jnp.einsum("te,de->td", d_branch, out_mat, preferred_element_type=jnp.float32)
        .astype(jnp.bfloat16)
        .reshape(head_shape)
    )
    d_attn_prob = jnp.einsum(
        "bqhd,bkhd->bhqk", d_att, saved["value_part"], preferred_element_type=jnp.float32
    )
    d_value = jnp.einsum(
        "bhqk,bqhd->bkhd", saved["prob_low"], d_att, preferred_element_type=jnp.float32
    )
    attn_prob = saved["attn_prob"]
    d_scores = (
        attn_prob * (d_attn_prob - jnp.sum(attn_prob * d_attn_prob, -1, keepdims=True))
    ).astype(jnp.bfloat16)
    d_query = (
        jnp.einsum(
            "bhqk,bkhd->bqhd", d_scores, saved["key_part"], preferred_element_type=jnp.float32
        )
        * scale_val
    )
    d_key = (
        jnp.einsum(
            "bhqk,bqhd->bkhd", d_scores, saved["query_part"], preferred_element_type=jnp.float32
        )
        * scale_val
    )
    d_proj = jnp.concatenate(
        [
            d_query.reshape(row_count, model_width),
            d_key.reshape(row_count, model_width),
            d_value.reshape(row_count, model_width),
        ],
        1,
    ).astype(jnp.bfloat16)
    d_proj_wide = d_proj.astype(jnp.float32)
    grad_qv = grad_list[3] + jnp.stack(
        [jnp.sum(d_proj_wide[:, :model_width], 0), jnp.sum(d_proj_wide[:, 2 * model_width :], 0)]
    )
    grad_qkv = grad_list[2] + jnp.einsum(
        "td,te->de", saved["normed"], d_proj, preferred_element_type=jnp.float32
    )
    d_normed = jnp.einsum("te,de->td", d_proj, qkv_mat, preferred_element_type=jnp.float32)
    first_value, first_pull = jax.vjp(
        layer_norm, flat_tok, gain_one.astype(jnp.float32), shift_one.astype(jnp.float32)
    )
    d_tok_norm, d_gain_one, d_shift_one = first_pull(d_normed)
    d_tokens = d_middle + d_tok_norm
    new_list = [
        grad_list[0] + d_gain_one,
        grad_list[1] + d_shift_one,
        grad_qkv,
        grad_qv,
        grad_out,
        grad_out_vec,
        grad_list[6] + d_gain_two,
        grad_list[7] + d_shift_two,
        grad_router,
        grad_inner,
        grad_inner_vec,
        grad_outer,
        grad_outer_vec,
    ]
    return (d_tokens.reshape(image_rows, seq_len, model_width), new_list)


def shards(
    images,
    image_count,
    expert_index,
    expert_slot,
    keep,
    cotangent,
    ln1_gain,
    ln1_bias,
    qkv_weight,
    qv_bias,
    out_weight,
    out_bias,
    ln2_gain,
    ln2_bias,
    router_weight,
    expert_in,
    expert_in_bias,
    expert_out,
    expert_out_bias,
):
    slot_total = images.shape[0]
    seq_len = images.shape[1]
    per_batch = slot_total // MICRO
    live_img = (jnp.arange(slot_total) < image_count[0]).astype(jnp.float32)
    live_all = jnp.repeat(live_img, seq_len)
    expert_hits = (
        expert_index.reshape(-1, 2)[:, :, None] == jnp.arange(EXPERTS)[None, None, :]
    ).astype(jnp.float32)
    local_counts = jnp.sum(expert_hits * live_all[:, None, None], axis=(0, 1))
    outputs = []
    prob_total = jnp.zeros((EXPERTS,), jnp.float32)
    for batch_index in range(MICRO):
        gathered = (
            lax.all_gather(ln1_gain, "dp", axis=0, tiled=True),
            lax.all_gather(ln1_bias, "dp", axis=0, tiled=True),
            lax.all_gather(qkv_weight, "dp", axis=0, tiled=True),
            lax.all_gather(qv_bias, "dp", axis=1, tiled=True),
            lax.all_gather(out_weight, "dp", axis=0, tiled=True),
            lax.all_gather(out_bias, "dp", axis=0, tiled=True),
            lax.all_gather(ln2_gain, "dp", axis=0, tiled=True),
            lax.all_gather(ln2_bias, "dp", axis=0, tiled=True),
            lax.all_gather(router_weight, "dp", axis=0, tiled=True),
            lax.all_gather(expert_in, "dp", axis=1, tiled=True),
            lax.all_gather(expert_in_bias, "dp", axis=1, tiled=True),
            lax.all_gather(expert_out, "dp", axis=1, tiled=True),
            lax.all_gather(expert_out_bias, "dp", axis=1, tiled=True),
        )
        lower = batch_index * per_batch
        upper = lower + per_batch
        live_tok = jnp.repeat(live_img[lower:upper], seq_len)
        saved = forward_pass(
            gathered,
            images[lower:upper],
            expert_index[lower:upper].reshape(-1, 2),
            expert_slot[lower:upper].reshape(-1, 2),
            keep[lower:upper].reshape(-1, 2),
            live_tok,
        )
        outputs.append(saved["result"].reshape(per_batch, seq_len, -1))
        prob_total = prob_total + jnp.sum(saved["router_prob"] * live_tok[:, None], axis=0)
    counts_all, live_total, prob_all = lax.psum((local_counts, jnp.sum(live_all), prob_total), "dp")
    balance = EXPERTS * jnp.sum(counts_all / live_total * prob_all / live_total)
    balance_coef = BALANCE_WEIGHT * EXPERTS * counts_all / live_total
    grad_list = [jnp.zeros(member.shape, jnp.float32) for member in gathered]
    input_grads = []
    for batch_index in range(MICRO):
        gathered = (
            lax.all_gather(ln1_gain, "dp", axis=0, tiled=True),
            lax.all_gather(ln1_bias, "dp", axis=0, tiled=True),
            lax.all_gather(qkv_weight, "dp", axis=0, tiled=True),
            lax.all_gather(qv_bias, "dp", axis=1, tiled=True),
            lax.all_gather(out_weight, "dp", axis=0, tiled=True),
            lax.all_gather(out_bias, "dp", axis=0, tiled=True),
            lax.all_gather(ln2_gain, "dp", axis=0, tiled=True),
            lax.all_gather(ln2_bias, "dp", axis=0, tiled=True),
            lax.all_gather(router_weight, "dp", axis=0, tiled=True),
            lax.all_gather(expert_in, "dp", axis=1, tiled=True),
            lax.all_gather(expert_in_bias, "dp", axis=1, tiled=True),
            lax.all_gather(expert_out, "dp", axis=1, tiled=True),
            lax.all_gather(expert_out_bias, "dp", axis=1, tiled=True),
        )
        lower = batch_index * per_batch
        upper = lower + per_batch
        live_tok = jnp.repeat(live_img[lower:upper], seq_len)
        routes = expert_index[lower:upper].reshape(-1, 2)
        kept_flag = keep[lower:upper].reshape(-1, 2)
        saved = forward_pass(
            gathered,
            images[lower:upper],
            routes,
            expert_slot[lower:upper].reshape(-1, 2),
            kept_flag,
            live_tok,
        )
        d_tokens, grad_list = backward_pass(
            gathered,
            saved,
            cotangent[lower:upper],
            live_tok,
            routes,
            kept_flag,
            balance_coef,
            grad_list,
        )
        input_grads.append(d_tokens)
    owned = (
        lax.psum_scatter(grad_list[0], "dp", scatter_dimension=0, tiled=True),
        lax.psum_scatter(grad_list[1], "dp", scatter_dimension=0, tiled=True),
        lax.psum_scatter(grad_list[2], "dp", scatter_dimension=0, tiled=True),
        lax.psum_scatter(grad_list[3], "dp", scatter_dimension=1, tiled=True),
        lax.psum_scatter(grad_list[4], "dp", scatter_dimension=0, tiled=True),
        lax.psum_scatter(grad_list[5], "dp", scatter_dimension=0, tiled=True),
        lax.psum_scatter(grad_list[6], "dp", scatter_dimension=0, tiled=True),
        lax.psum_scatter(grad_list[7], "dp", scatter_dimension=0, tiled=True),
        lax.psum_scatter(grad_list[8], "dp", scatter_dimension=0, tiled=True),
        lax.psum_scatter(grad_list[9], "dp", scatter_dimension=1, tiled=True),
        lax.psum_scatter(grad_list[10], "dp", scatter_dimension=1, tiled=True),
        lax.psum_scatter(grad_list[11], "dp", scatter_dimension=1, tiled=True),
        lax.psum_scatter(grad_list[12], "dp", scatter_dimension=1, tiled=True),
    )
    block_out = jnp.concatenate(outputs, 0).astype(jnp.bfloat16)
    image_grad = jnp.concatenate(input_grads, 0).astype(jnp.bfloat16)
    return (
        block_out,
        image_grad,
        balance,
        owned[0],
        owned[1],
        owned[2],
        owned[3],
        owned[4],
        owned[5],
        owned[6],
        owned[7],
        owned[8],
        owned[9],
        owned[10],
        owned[11],
        owned[12],
    )


def solution(mesh):
    placed = (
        P("dp", None, None),
        P("dp"),
        P("dp", None, None),
        P("dp", None, None),
        P("dp", None, None),
        P("dp", None, None),
        P("dp"),
        P("dp"),
        P("dp", None),
        P(None, "dp"),
        P("dp", None),
        P("dp"),
        P("dp"),
        P("dp"),
        P("dp", None),
        P(None, "dp", None),
        P(None, "dp"),
        P(None, "dp", None),
        P(None, "dp"),
    )
    return jax.shard_map(
        shards,
        mesh=mesh,
        in_specs=placed,
        out_specs=(
            P("dp", None, None),
            P("dp", None, None),
            P(),
            P("dp"),
            P("dp"),
            P("dp", None),
            P(None, "dp"),
            P("dp", None),
            P("dp"),
            P("dp"),
            P("dp"),
            P("dp", None),
            P(None, "dp", None),
            P(None, "dp"),
            P(None, "dp", None),
            P(None, "dp"),
        ),
        check_vma=False,
    )
```

profile of v0, /device:TPU:0, one launch (start us, length us, event | category | flops | bytes accessed | tf_op | source)
XLA Modules:
  0.0 2555.9 jit_solution(3727828375674264795)
XLA Ops:
  11.9 42.3 %all-reduce.19 = (f32[8]{0:T(128)}, f32[]{:T(128)}) all-reduce(f32[8]{0:T(128)S(1)} %select_reduce_fusion, f32[]{:T(128)} %broadcast_reduce_fusion), channel_id=1, replica_groups=mesh['dp'=32] {'dp'}, use_global_device_ids=true, to_apply=%region_45.47 | all-reduce | flops 9 | bytes 72 | tf_op jit(solution)/shard_map/psum | solution.py:333
  64.2 41.3 %all-reduce.20 = (bf16[512]{0:T(512)(128)(2,1)S(1)}, bf16[512]{0:T(512)(128)(2,1)S(1)}, bf16[512]{0:T(512)(128)(2,1)S(1)}, bf16[512]{0:T(512)(128)(2,1)S(1)}, bf16[512]{0:T(512)(128)(2,1)S(1)}) all-reduce(bf16[512]{0:T(512)(128)(2,1)S(1)} %dynamic-update-slice.1, ...), channel_id=1, replica_groups=mesh['dp'=32] {'dp'}, use_global_device_ids=true, to_apply=%add.9 | all-reduce | flops 2560 | bytes 10240
  113.7 40.9 %all-gather = bf16[32,16,2]{1,2,0:T(2,128)(2,1)S(1)} all-gather(bf16[1,16,2]{1,2,0:T(2,128)(2,1)S(1)} %bitcast.379), channel_id=1, replica_groups=mesh['dp'=32] {'dp'}, dimensions={0}, use_global_device_ids=true | all-gather | bytes 2112 | tf_op jit(solution)/shard_map/all_gather | solution.py:309
  168.0 37.6 %all-gather.2 = bf16[32,64,8]{1,2,0:T(8,128)(2,1)S(1)} all-gather(bf16[1,64,8]{1,2,0:T(8,128)(2,1)S(1)} %bitcast.376), channel_id=1, replica_groups=mesh['dp'=32] {'dp'}, dimensions={0}, use_global_device_ids=true | all-gather | bytes 33792 | tf_op jit(solution)/shard_map/all_gather | solution.py:316
  231.6 39.0 %all-gather.1 = bf16[32,16,8]{1,2,0:T(8,128)(2,1)S(1)} all-gather(bf16[1,16,8]{1,2,0:T(8,128)(2,1)S(1)} %bitcast.377), channel_id=1, replica_groups=mesh['dp'=32] {'dp'}, dimensions={0}, use_global_device_ids=true | all-gather | bytes 8448 | tf_op jit(solution)/shard_map/all_gather | solution.py:314
  299.3 36.8 %all-gather.3 = bf16[32,16,8]{1,2,0:T(8,128)(2,1)S(1)} all-gather(bf16[1,16,8]{1,2,0:T(8,128)(2,1)S(1)} %bitcast.378), channel_id=1, replica_groups=mesh['dp'=32] {'dp'}, dimensions={0}, use_global_device_ids=true | all-gather | bytes 8448 | tf_op jit(solution)/shard_map/all_gather | solution.py:318
  357.3 39.4 %all_gather.30 = bf16[512,512]{1,0:T(8,128)(2,1)S(1)} all-gather(bf16[16,512]{1,0:T(8,128)(2,1)S(1)} %copy-done.275), channel_id=1, replica_groups=mesh['dp'=32] {'dp'}, dimensions={0}, use_global_device_ids=true | all-gather | bytes 540672 | tf_op jit(solution)/shard_map/all_gather | solution.py:310
  639.5 12.6 fusion.196
  664.4 14.6 fusion.202
  679.0 25.8 %fusion.48 = (u8[128,2048]{1,0:T(8,128)(4,1)}, u8[128,2048]{1,0:T(8,128)(4,1)}, u8[128,2048]{1,0:T(8,128)(4,1)}, u8[128,2048]{1,0:T(8,128)(4,1)}, u8[128,2048]{1...) fusion(f32[8,2048]{1,0:T(8,128)} %bitcast.357, ...), kind=kOutput, calls=%fused_computation.154 | convolution fusion | flops 2262827008 | bytes 53542912 | tf_op jit(solution)/shard_map/ecd,edf->ecf/dot_general | solution.py:94
  704.7 50.8 %convert_reduce_fusion.1 = (f32[8,2048]{1,0:T(8,128)}, bf16[8,128,2048]{2,1,0:T(8,128)(2,1)}, f32[8,128,2048]{2,1,0:T(8,128)}, f32[8,2048]{1,0:T(8,128)}, bf16[8...) fusion(f32[8,128,2048]{2,1,0:T(8,128)} %fusion.195, f32[8,2048]{1,0:T(8,128)} %bitcast.358, ...), kind=kOutput, calls=%fused_computation.52 | convolution fusion | flops 2480898048 | bytes 69402624 | tf_op jit(solution)/shard_map/ecd,efd->ecf/dot_general | solution.py:171
  755.5 33.7 %convert_reduce_fusion.3 = (f32[8,2048]{1,0:T(8,128)}, bf16[8,128,2048]{2,1,0:T(8,128)(2,1)}, f32[8,128,2048]{2,1,0:T(8,128)}, bf16[8,128,2048]{2,1,0:T(8,128)(2,1)S(1)}, bf16[8,128,2048]{2,1,0:T(8,128)(2,1)}) fusion(f32[8,128,2048]{2,1,0:T(8,128)} %get-tuple-element.309, f32[8,2048]{1,0:T(8,128)} %bitcast.359, u8[128,2048]{1,0:T(8,128)(4,1)} %get-tuple-element.82, ...), kind=kOutput, calls=%fused_computation.54 | convolution fusion | flops 2332016640 | bytes 81395712 | tf_op jit(solution)/shard_map/ecd,efd->ecf/dot_general | solution.py:171
  831.8 14.1 fusion.200
  858.6 30.9 %convert_reduce_fusion.2 = (f32[8,2048]{1,0:T(8,128)}, bf16[8,128,2048]{2,1,0:T(8,128)(2,1)}, f32[8,128,2048]{2,1,0:T(8,128)}, bf16[8,128,2048]{2,1,0:T(8,128)(2,1)}) fusion(f32[8,128,2048]{2,1,0:T(8,128)} %fusion.194, f32[8,2048]{1,0:T(8,128)S(1)} %bitcast.360, u8[128,2048]{1,0:T(8,128)(4,1)S(1)} %copy-done.313, u8[128,2048]{1,0:T(8,128)(4,1)S(1)} %copy-done.314, ...), kind=kOutput, calls=%fused_computation.53 | convolution fusion | flops 2323628032 | bytes 60424192 | tf_op jit(solution)/shard_map/ecd,efd->ecf/dot_general | solution.py:171
  946.6 14.1 fusion.203
  971.5 14.1 fusion.197
  1005.0 14.1 fusion.198
  1111.5 13.3 fusion.207
  1124.8 13.1 fusion.205
  1204.0 15.4 fusion.206
  1219.5 44.8 %add_add_fusion.1 = f32[8,512,2048]{2,1,0:T(8,128)} fusion(f32[8,512,2048]{2,1,0:T(8,128)} %fusion.207, f32[8,512,2048]{2,1,0:T(8,128)} %fusion.205, f32[8,512,2048]{2,1,0:T(8,128)} %fusion.206, bf16[8,128,512]{2,1,0:T(8,128)(2,1)S(1)} %bitcast.337, bf16[8,128,2048]{2,1,0:T(8,128)(2,1)} %get-tuple-element.236), kind=kOutput, calls=%fused_computation.25 | convolution fusion | flops 2172649472 | bytes 139460608 | tf_op jit(solution)/shard_map/ecd,ecf->edf/dot_general | solution.py:175
  1265.5 15.5 fusion.210
  1281.1 18.3 fusion.208
  1299.4 14.4 fusion.209
  1313.7 45.0 %add_add_fusion = f32[8,2048,512]{2,1,0:T(8,128)} fusion(f32[8,2048,512]{2,1,0:T(8,128)} %fusion.210, f32[8,2048,512]{2,1,0:T(8,128)} %fusion.208, f32[8,2048,512]{2,1,0:T(8,128)} %fusion.209, bf16[8,128,2048]{2,1,0:T(8,128)(2,1)} %copy-done.35, bf16[8,128,512]{2,1,0:T(8,128)(2,1)} %bitcast.331), kind=kOutput, calls=%fused_computation.24 | convolution fusion | flops 2172649472 | bytes 139460608 | tf_op jit(solution)/shard_map/ecf,ecd->efd/dot_general | solution.py:168
  1369.9 37.1 %all-reduce.18 = (f32[8]{0:T(128)S(1)}, f32[512]{0:T(512)S(1)}, f32[512]{0:T(512)S(1)}, f32[512]{0:T(512)S(1)}, f32[512]{0:T(512)S(1)}, /*index=5*/f32[512]{0:T(512)S(1)}) all-reduce(f32[8]{0:T(128)S(1)} %add_add_fusion.21, f32[512]{0:T(512)S(1)} %add_add_fusion.20, f32[512]{0:T(512)S(1)} %add_add_fusion.19, ...), channel_id=1, replica_groups=mesh['dp'=32] {'dp'}, use_global_device_ids=true, to_apply=%region_88.90 | all-reduce | flops 2568 | bytes 20544 | tf_op jit(solution)/shard_map/psum | solution.py:333
  1436.2 19.8 reduce-scatter.27.cloned.1.call-done
  1457.3 131.8 %reduce-scatter.29.cloned.1.call-done = f32[64,8]{1,0:T(8,128)} async-done(((f32[2048,8]{1,0:T(8,128)}), f32[64,8]{1,0:T(8,128)}) %reduce-scatter.29.cloned.1.call-update) | async-done | bytes 2064
  1590.5 132.1 %reduce-scatter.19.cloned.1.call-done = f32[16,512]{1,0:T(8,128)} async-done(((f32[512,512]{1,0:T(8,128)}), f32[16,512]{1,0:T(8,128)}) %reduce-scatter.19.cloned.1.call-update) | async-done | bytes 32784 | tf_op jit(solution)/shard_map/reduce_scatter | solution.py:383
  1722.6 104.4 %reduce-scatter.17.cloned.1.call-done = f32[16,1536]{1,0:T(8,128)} async-done(((f32[512,1536]{1,0:T(8,128)}), f32[16,1536]{1,0:T(8,128)}) %reduce-scatter.17.cloned.1.call-update) | async-done | bytes 98320 | tf_op jit(solution)/shard_map/reduce_scatter | solution.py:381
  1827.0 356.1 %reduce-scatter.21.cloned.1.call-done = f32[8,16,2048]{2,1,0:T(8,128)} async-done(((f32[8,512,2048]{2,1,0:T(8,128)}), f32[8,16,2048]{2,1,0:T(8,128)}) %reduce-scatter.21.cloned.1.call-update) | async-done | bytes 1048592 | tf_op jit(solution)/shard_map/reduce_scatter | solution.py:388
  2183.1 364.9 %reduce-scatter.23.cloned.1.call-done = f32[8,64,512]{2,1,0:T(8,128)} async-done(((f32[8,2048,512]{2,1,0:T(8,128)}), f32[8,64,512]{2,1,0:T(8,128)}) %reduce-scatter.23.cloned.1.call-update) | async-done | bytes 1048592 | tf_op jit(solution)/shard_map/reduce_scatter | solution.py:390
  (1161 shorter events, 707.4 us)
Async XLA Ops:
  7.2 389.6 %all-gather.8.cloned.1.call-start = ((), (), s32[]{:S(2)}) async-start(), calls=%async_computation.8 | async-start | bytes 1622016 | tf_op jit(solution)/shard_map/all_gather | solution.py:308
  7.9 631.5 %all-gather.10.cloned.1.call-start = ((), (), s32[]{:S(2)}) async-start(), calls=%async_computation.9 | async-start | bytes 17301504 | tf_op jit(solution)/shard_map/all_gather | solution.py:315
  8.7 655.7 %all-gather.12.cloned.1.call-start = ((), (), s32[]{:S(2)}) async-start(), calls=%async_computation.10 | async-start | bytes 17301504 | tf_op jit(solution)/shard_map/all_gather | solution.py:317
  9.4 1349.5 %reduce-scatter.31.cloned.1.call-start = ((), (), s32[]{:S(2)}) async-start(), calls=%async_computation.18 | async-start | bytes 270336
  58.0 55.7 %copy-start.310 = (bf16[2,16]{1,0:T(2,128)(2,1)S(1)}, bf16[2,16]{1,0:T(2,128)(2,1)}, u32[]{:S(2)}) copy-start(bf16[2,16]{1,0:T(2,128)(2,1)} %param.30) | copy-start | bytes 196
  58.6 96.1 %copy-start.37 = (bf16[8,197,512]{2,0,1:T(8,128)(2,1)S(1)}, bf16[8,197,512]{2,0,1:T(8,128)(2,1)}, u32[]{:S(2)}) copy-start(bf16[8,197,512]{2,0,1:T(8,128)(2,1)} %param.21) | copy-start | bytes 4841476
  113.6 390.6 %copy-start.14 = (f32[394,512]{1,0:T(8,128)}, f32[394,512]{1,0:T(8,128)S(1)}, u32[]{:S(2)}) copy-start(f32[394,512]{1,0:T(8,128)S(1)} %reshape.1298) | copy-start | bytes 2420740
  162.5 234.3 %copy-start.216 = (f32[394]{0:T(512)}, f32[394]{0:T(512)S(1)}, u32[]{:S(2)}) copy-start(f32[394]{0:T(512)S(1)} %rsqrt.98) | copy-start | bytes 4732
  162.6 234.2 %copy-start.219 = (f32[394]{0:T(512)}, f32[394]{0:T(512)S(1)}, u32[]{:S(2)}) copy-start(f32[394]{0:T(512)S(1)} %div.304) | copy-start | bytes 4732
  162.6 313.2 %copy-start.190 = (f32[512]{0:T(512)}, f32[512]{0:T(512)S(1)}, u32[]{:S(2)}) copy-start(f32[512]{0:T(512)S(1)} %convert_element_type.474) | copy-start | bytes 6148
  162.6 313.2 %copy-start.161 = (f32[512]{0:T(512)}, f32[512]{0:T(512)S(1)}, u32[]{:S(2)}) copy-start(f32[512]{0:T(512)S(1)} %convert_element_type.473) | copy-start | bytes 6148
  162.6 347.3 %copy-start.174 = (f32[512]{0:T(512)}, f32[512]{0:T(512)S(1)}, u32[]{:S(2)}) copy-start(f32[512]{0:T(512)S(1)} %convert_element_type.485) | copy-start | bytes 6148
  163.4 61.0 %copy-start.164 = (f32[394]{0:T(512)}, f32[394]{0:T(512)S(1)}, u32[]{:S(2)}) copy-start(f32[394]{0:T(512)S(1)} %mul.1297) | copy-start | bytes 4732
  209.9 296.2 %copy-start.17 = (f32[394,512]{1,0:T(8,128)}, f32[394,512]{1,0:T(8,128)S(1)}, u32[]{:S(2)}) copy-start(f32[394,512]{1,0:T(8,128)S(1)} %reshape.1299) | copy-start | bytes 2420740
  210.1 237.1 %copy-start.222 = (f32[394]{0:T(512)}, f32[394]{0:T(512)S(1)}, u32[]{:S(2)}) copy-start(f32[394]{0:T(512)S(1)} %rsqrt.100) | copy-start | bytes 4732
  210.3 237.0 %copy-start.225 = (f32[394]{0:T(512)}, f32[394]{0:T(512)S(1)}, u32[]{:S(2)}) copy-start(f32[394]{0:T(512)S(1)} %div.313) | copy-start | bytes 4732
  213.7 295.3 %copy-start.20 = (f32[394,512]{1,0:T(8,128)}, f32[394,512]{1,0:T(8,128)S(1)}, u32[]{:S(2)}) copy-start(f32[394,512]{1,0:T(8,128)S(1)} %reshape.1295) | copy-start | bytes 2420740
  231.6 326.1 %copy-start.208 = (f32[394,2]{0,1:T(2,128)}, f32[394,2]{0,1:T(2,128)S(1)}, u32[]{:S(2)}) copy-start(f32[394,2]{0,1:T(2,128)S(1)} %convert_element_type.528) | copy-start | bytes 9460
  270.7 308.4 %copy-start.146 = (bf16[512,8]{0,1:T(8,128)(2,1)}, bf16[512,8]{0,1:T(8,128)(2,1)S(1)}, u32[]{:S(2)}) copy-start(bf16[512,8]{0,1:T(8,128)(2,1)S(1)} %reshape.1498) | copy-start | bytes 24580
  270.9 286.9 %copy-start.179 = (s32[394,2]{0,1:T(2,128)}, s32[394,2]{0,1:T(2,128)S(1)}, u32[]{:S(2)}) copy-start(s32[394,2]{0,1:T(2,128)S(1)} %reshape.1263) | copy-start | bytes 9460
  396.7 112.3 %copy-start.4 = (bf16[512,512]{1,0:T(8,128)(2,1)}, bf16[512,512]{1,0:T(8,128)(2,1)S(1)}, u32[]{:S(2)}) copy-start(bf16[512,512]{1,0:T(8,128)(2,1)S(1)} %all_gather.30) | copy-start | bytes 1572868
  447.2 60.9 %copy-start.98 = (bf16[394,512]{0,1:T(8,128)(2,1)}, bf16[394,512]{0,1:T(8,128)(2,1)S(1)}, u32[]{:S(2)}) copy-start(bf16[394,512]{0,1:T(8,128)(2,1)S(1)} %reshape.1262) | copy-start | bytes 1210372
  510.8 58.1 %copy-start.87 = (bf16[394,512]{1,0:T(8,128)(2,1)}, bf16[394,512]{1,0:T(8,128)(2,1)S(1)}, u32[]{:S(2)}) copy-start(bf16[394,512]{1,0:T(8,128)(2,1)S(1)} %get-tuple-element.252) | copy-start | bytes 1210372
  632.2 72.5 %copy-start.89 = (bf16[1024,512]{1,0:T(8,128)(2,1)}, bf16[1024,512]{1,0:T(8,128)(2,1)S(1)}, u32[]{:S(2)}) copy-start(bf16[1024,512]{1,0:T(8,128)(2,1)S(1)} %get-tuple-element.169) | copy-start | bytes 3145732
  639.2 795.6 %reduce-scatter.25.cloned.1.call-start = ((), (), s32[]{:S(2)}) async-start(), calls=%async_computation.15 | async-start | bytes 270336
  1036.7 160.3 %copy-start.41 = (f32[394,512]{1,0:T(8,128)}, f32[394,512]{1,0:T(8,128)S(1)}, u32[]{:S(2)}) copy-start(f32[394,512]{1,0:T(8,128)S(1)} %get-tuple-element.189) | copy-start | bytes 2420740
  1194.9 261.0 %reduce-scatter.27.cloned.1.call-start = ((), (), s32[]{:S(2)}) async-start(), calls=%async_computation.16 | async-start | bytes 270336
  1196.0 393.0 %reduce-scatter.29.cloned.1.call-start = ((), (), s32[]{:S(2)}) async-start(), calls=%async_computation.17 | async-start | bytes 1081344
  1201.2 521.4 %reduce-scatter.19.cloned.1.call-start = ((), (), s32[]{:S(2)}) async-start(), calls=%async_computation.12 | async-start | bytes 1081344 | tf_op jit(solution)/shard_map/reduce_scatter | solution.py:383
  1204.0 623.1 %reduce-scatter.17.cloned.1.call-start = ((), (), s32[]{:S(2)}) async-start(), calls=%async_computation.11 | async-start | bytes 3244032 | tf_op jit(solution)/shard_map/reduce_scatter | solution.py:381
  1219.5 963.7 %reduce-scatter.21.cloned.1.call-start = ((), (), s32[]{:S(2)}) async-start(), calls=%async_computation.13 | async-start | bytes 34603008 | tf_op jit(solution)/shard_map/reduce_scatter | solution.py:388
  1264.3 1283.7 %reduce-scatter.23.cloned.1.call-start = ((), (), s32[]{:S(2)}) async-start(), calls=%async_computation.14 | async-start | bytes 34603008 | tf_op jit(solution)/shard_map/reduce_scatter | solution.py:390
  (295 other events, 2397.8 us)
Sparse Core Ops, SparseCore 0:
  10.9 57.6 all-gather.7
  71.5 114.5 all-gather.9
  189.1 113.0 all-gather.11
  639.3 129.6 reduce-scatter.30
  1195.1 129.2 reduce-scatter.24
  1326.5 129.4 reduce-scatter.26
  1458.2 130.7 reduce-scatter.28
  1591.8 130.7 reduce-scatter.18
  1729.5 97.4 reduce-scatter.16
  1829.8 353.2 reduce-scatter.20
  2186.1 361.8 reduce-scatter.22
where the time goes:
time: 2570 us; the launch traced here: 2560 us
  waiting for transfers between devices  1110 us (43%)
  matrix products  568 us (22%)
  local copies, waits for them, and re-layouts  377 us (15%)
  blocking collectives  314 us (12%)
  other arithmetic  164 us (6%)
    reduce_scatter x1, waiting for transfers between devices, shards(): lax.psum_scatter(grad_list[11], 'dp', scatter_dimension=1, tiled=True)  365 us
    reduce_scatter x1, waiting for transfers between devices, shards(): lax.psum_scatter(grad_list[9], 'dp', scatter_dimension=1, tiled=True)  356 us
    unnamed x15, waiting for transfers between devices  154 us
    reduce_scatter x1, waiting for transfers between devices, shards(): lax.psum_scatter(grad_list[4], 'dp', scatter_dimension=0, tiled=True)  132 us
    dot_general x4, matrix products, backward_pass(): jnp.einsum('ecd,efd->ecf', d_res_low, outer_mat, preferred_element_type=j...  130 us
    reduce_scatter x1, waiting for transfers between devices, shards(): lax.psum_scatter(grad_list[2], 'dp', scatter_dimension=0, tiled=True)  104 us
    dot_general x4, matrix products, backward_pass(): jnp.einsum('ecf,ecd->efd', saved['activated'], d_res_low, preferred_eleme...  93.3 us
    dot_general x4, matrix products, backward_pass(): jnp.einsum('ecd,ecf->edf', saved['expert_rows'], d_hidden, preferred_elem...  86.5 us
  transfers between devices with their start and end apart: 11, of which 6 were waited for; matrix products, arithmetic and copies ran while one was open for 43% of the time, Pallas kernels for 0%

commit v1 on v0

v1 whole, which is shorter than its diff:
```python
import functools
import math

import jax
import jax.numpy as jnp
from jax import lax
from jax.experimental import pallas as pl
from jax.experimental.pallas import tpu as pltpu
from jax.sharding import PartitionSpec as P

HEADS = 8
HEAD_DIM = 64
EXPERTS = 8
MICRO = 4
CAP = 128
PAIR = 2 * HEAD_DIM

EPSILON = 1e-06
BALANCE_WEIGHT = 8.0

BF = jnp.bfloat16
F32 = jnp.float32

ROW_GAIN1, ROW_BIAS1, ROW_QBIAS, ROW_VBIAS, ROW_OBIAS, ROW_GAIN2, ROW_BIAS2 = range(8, 15)
SMALL = 128
GRAD_ROWS = 16
COL_T0, COL_T1, COL_R0, COL_R1, COL_K0, COL_K1, COL_LIVE = range(7)
VMEM_LIMIT = 60 * 1024 * 1024


def mm(a, b):
    return lax.dot_general(a, b, (((1,), (0,)), ((), ())), preferred_element_type=F32)


def mm_nt(a, b):
    return lax.dot_general(a, b, (((1,), (1,)), ((), ())), preferred_element_type=F32)


def mm_tn(a, b):
    return lax.dot_general(a, b, (((0,), (0,)), ((), ())), preferred_element_type=F32)


def load_padded(dst, src, seq_len, pad_len):
    for i in range(2):
        tail = (seq_len // 16) * 16
        dst[i * pad_len + tail : (i + 1) * pad_len, :] = jnp.zeros(
            (pad_len - tail, dst.shape[1]), dst.dtype
        )
        dst[i * pad_len : i * pad_len + seq_len, :] = src[i].astype(dst.dtype)


def norm_parts(x):
    mean = jnp.mean(x, -1, keepdims=True)
    centered = x - mean
    spread = jnp.mean(centered * centered, -1, keepdims=True)
    inv = lax.rsqrt(spread + EPSILON)
    return centered * inv, inv


def norm_back(d_out, xhat, inv, gain):
    d_hat = d_out * gain
    first = jnp.mean(d_hat, -1, keepdims=True)
    second = jnp.mean(d_hat * xhat, -1, keepdims=True)
    return inv * (d_hat - first - xhat * second)


def half_masks():
    lane = lax.broadcasted_iota(jnp.int32, (1, PAIR), 1)
    low = jnp.where(lane < HEAD_DIM, 1.0, 0.0)
    return low.astype(BF), (1.0 - low).astype(BF), lane < HEAD_DIM


def stack_heads(block, low, high):
    return jnp.concatenate([block * low, block * high], 0)


def forward_kernel(
    m0,
    seq_len,
    pad_len,
    cnt_ref,
    img_ref,
    cot_ref,
    lane_ref,
    meta_ref,
    w_ref,
    small_ref,
    xd_ref,
    qkv_ref,
    p_ref,
    att_ref,
    mid_ref,
    rp_ref,
    psum_ref,
    xs,
    cs,
):
    step = pl.program_id(0)
    width = xs.shape[1]
    alive = cnt_ref[0] > 2 * (m0 + step)

    @pl.when(step == 0)
    def _():
        psum_ref[...] = jnp.zeros_like(psum_ref)

    @pl.when(jnp.logical_not(alive))
    def _():
        xd_ref[...] = jnp.zeros_like(xd_ref)

    @pl.when(alive)
    def _():
        load_padded(xs, img_ref, seq_len, pad_len)
        load_padded(cs, cot_ref, seq_len, pad_len)
        xhat, inv = norm_parts(xs[...])
        normed = (
            xhat * small_ref[ROW_GAIN1 : ROW_GAIN1 + 1, :] + small_ref[ROW_BIAS1 : ROW_BIAS1 + 1, :]
        ).astype(BF)
        for part, row in ((0, ROW_QBIAS), (1, None), (2, ROW_VBIAS)):
            cols = slice(part * width, (part + 1) * width)
            value = mm(normed, w_ref[:, cols])
            if row is not None:
                value = value + small_ref[row : row + 1, :]
            qkv_ref[0, :, cols] = value.astype(BF)
        low, high, low_mask = half_masks()
        key_ok = lax.broadcasted_iota(jnp.int32, (1, pad_len), 1) < seq_len
        for i in range(2):
            rows = slice(i * pad_len, (i + 1) * pad_len)
            for hp in range(HEADS // 2):
                at = hp * PAIR
                q = qkv_ref[0, rows, at : at + PAIR]
                k = qkv_ref[0, rows, width + at : width + at + PAIR]
                v = qkv_ref[0, rows, 2 * width + at : 2 * width + at + PAIR]
                s = mm_nt(stack_heads(q, low, high), k) * (HEAD_DIM**-0.5)
                s = jnp.where(key_ok, s, -1e30)
                e = jnp.exp(s - jnp.max(s, -1, keepdims=True))
                p = (e * (1.0 / jnp.sum(e, -1, keepdims=True))).astype(BF)
                p_ref[0, i, hp] = p
                o = mm(p, v)
                att_ref[0, rows, at : at + PAIR] = jnp.where(
                    low_mask, o[:pad_len], o[pad_len:]
                ).astype(BF)
        middle = (
            xs[...]
            + mm(att_ref[0], w_ref[:, 3 * width : 4 * width])
            + small_ref[ROW_OBIAS : ROW_OBIAS + 1, :]
        )
        mid_ref[0] = middle
        xhat2, inv2 = norm_parts(middle)
        mixed = (
            xhat2 * small_ref[ROW_GAIN2 : ROW_GAIN2 + 1, :]
            + small_ref[ROW_BIAS2 : ROW_BIAS2 + 1, :]
        ).astype(BF)
        logits = mm(mixed, w_ref[:, 4 * width : 4 * width + SMALL])
        lane = lax.broadcasted_iota(jnp.int32, (1, SMALL), 1)
        logits = jnp.where(lane < EXPERTS, logits, -1e30)
        e = jnp.exp(logits - jnp.max(logits, -1, keepdims=True))
        rp = e * (1.0 / jnp.sum(e, -1, keepdims=True))
        rp_ref[0] = rp
        live = meta_ref[0, :, COL_LIVE : COL_LIVE + 1]
        psum_ref[0:1, :] += jnp.sum(rp * live, 0, keepdims=True)
        d_final = cs[...] * live
        lane_f = lane.astype(F32)
        weighted = []
        for route, kept in ((COL_R0, COL_K0), (COL_R1, COL_K1)):
            hot = lane_f == meta_ref[0, :, route : route + 1]
            gate = jnp.sum(jnp.where(hot, rp, 0.0), -1, keepdims=True)
            gate = gate * meta_ref[0, :, kept : kept + 1]
            weighted.append((gate * d_final).astype(BF))
        slot = lax.broadcasted_iota(jnp.int32, (CAP, 1), 0).astype(F32)
        for e_id in range(EXPERTS):
            here = slot + float(e_id * CAP)
            sel0 = jnp.where(here == lane_ref[0, 0:1, :], 1.0, 0.0)
            sel1 = jnp.where(here == lane_ref[0, 1:2, :], 1.0, 0.0)
            xd_ref[e_id, 0, 0] = mm((sel0 + sel1).astype(BF), mixed).astype(BF)
            xd_ref[e_id, 1, 0] = (
                mm(sel0.astype(BF), weighted[0]) + mm(sel1.astype(BF), weighted[1])
            ).astype(BF)


def full_block(shape):
    return pl.BlockSpec(shape, lambda i: (0,) * len(shape))


def forward_call(m0, mbc, images, cotangent, count, lane_t, meta, weights, small):
    seq_len, width = images.shape[1], images.shape[2]
    rows = meta.shape[1]
    pad_len = rows // 2
    at = lambda i: i + m0
    mb = images.shape[0] // MICRO
    return pl.pallas_call(
        functools.partial(forward_kernel, m0, seq_len, pad_len),
        grid=(mbc,),
        in_specs=[
            pl.BlockSpec(memory_space=pltpu.SMEM),
            pl.BlockSpec((mb, seq_len, width), lambda i: (at(i), 0, 0)),
            pl.BlockSpec((mb, seq_len, width), lambda i: (at(i), 0, 0)),
            pl.BlockSpec((1, 8, rows), lambda i: (at(i), 0, 0)),
            pl.BlockSpec((1, rows, 8), lambda i: (at(i), 0, 0)),
            full_block(weights.shape),
            full_block(small.shape),
        ],
        out_specs=[
            pl.BlockSpec((EXPERTS, 2, 1, CAP, width), lambda i: (0, 0, i, 0, 0)),
            pl.BlockSpec((1, rows, 3 * width), lambda i: (i, 0, 0)),
            pl.BlockSpec((1, 2, HEADS // 2, rows, pad_len), lambda i: (i, 0, 0, 0, 0)),
            pl.BlockSpec((1, rows, width), lambda i: (i, 0, 0)),
            pl.BlockSpec((1, rows, width), lambda i: (i, 0, 0)),
            pl.BlockSpec((1, rows, SMALL), lambda i: (i, 0, 0)),
            full_block((8, SMALL)),
        ],
        out_shape=[
            jax.ShapeDtypeStruct((EXPERTS, 2, mbc, CAP, width), BF),
            jax.ShapeDtypeStruct((mbc, rows, 3 * width), BF),
            jax.ShapeDtypeStruct((mbc, 2, HEADS // 2, rows, pad_len), BF),
            jax.ShapeDtypeStruct((mbc, rows, width), BF),
            jax.ShapeDtypeStruct((mbc, rows, width), F32),
            jax.ShapeDtypeStruct((mbc, rows, SMALL), F32),
            jax.ShapeDtypeStruct((8, SMALL), F32),
        ],
        scratch_shapes=[pltpu.VMEM((rows, width), F32), pltpu.VMEM((rows, width), F32)],
        compiler_params=pltpu.CompilerParams(vmem_limit_bytes=VMEM_LIMIT),
        cost_estimate=pl.CostEstimate(
            flops=mbc * 12 * 10**9, bytes_accessed=mbc * 10 * 10**6, transcendentals=0
        ),
        name="dense_forward",
    )(count, images, cotangent, lane_t, meta, weights, small)


GROUP = 4
FF_TILE = 512


def expert_kernel(
    m0,
    mbc,
    has_acc,
    last,
    cnt_ref,
    x_ref,
    w1_ref,
    w2_ref,
    b1_ref,
    b2_ref,
    *rest,
):
    if has_acc:
        a1_ref, a2_ref, ab1_ref, ab2_ref = rest[:4]
        rest = rest[4:]
    y_ref, g1_ref, g2_ref, gb1_ref, gb2_ref = rest[:5]
    rest = rest[5:]
    if last:
        s1, s2, order, xin, din, xout, dout = rest
    else:
        order, xin, din, xout, dout = rest
        s1, s2 = g1_ref, g2_ref
    width = x_ref.shape[-1]
    ff = w1_ref.shape[1]
    if has_acc:
        s1[...] = a1_ref[...]
        s2[...] = a2_ref[...]
        gb1_ref[...] = ab1_ref[...]
        gb2_ref[...] = ab2_ref[...]
    else:
        s1[...] = jnp.zeros_like(s1)
        s2[...] = jnp.zeros_like(s2)
        gb1_ref[...] = jnp.zeros_like(gb1_ref)
        gb2_ref[...] = jnp.zeros_like(gb2_ref)
    blocks = EXPERTS * mbc

    def is_live(b):
        return (cnt_ref[b // mbc] > 2 * (m0 + b % mbc)).astype(jnp.int32)

    live_total = jnp.int32(0)
    for b in range(blocks):
        live_total = live_total + is_live(b)
    head, tail = jnp.int32(0), live_total
    for b in range(blocks):
        flag = is_live(b)
        order[jnp.where(flag == 1, head, tail)] = b
        head = head + flag
        tail = tail + (1 - flag)

    def one_group(g, carry):
        for j in range(GROUP):
            b = order[g * GROUP + j]
            xin[j * CAP : (j + 1) * CAP, :] = x_ref[b // mbc, 0, b % mbc]
            din[j * CAP : (j + 1) * CAP, :] = x_ref[b // mbc, 1, b % mbc]
        rows_in, d_res = xin[...], din[...]
        gb2_ref[0:1, :] += jnp.sum(d_res.astype(F32), 0, keepdims=True)
        for f in range(ff // FF_TILE):
            cols = slice(f * FF_TILE, (f + 1) * FF_TILE)
            w1 = w1_ref[:, cols]
            w2 = w2_ref[cols, :]
            h = mm(rows_in, w1) + b1_ref[0:1, cols]
            bell = jnp.exp(-0.5 * h * h)
            t = 1.0 / (1.0 + (0.3275911 / math.sqrt(2.0)) * jnp.abs(h))
            poly = t * (
                0.5 * 0.254829592
                + t
                * (
                    0.5 * -0.284496736
                    + t * (0.5 * 1.421413741 + t * (0.5 * -1.453152027 + t * (0.5 * 1.061405429)))
                )
            )
            upper = poly * bell
            cdf = jnp.where(h < 0.0, upper, 1.0 - upper)
            act = (h * cdf).astype(BF)
            slope = cdf + h * bell * (1.0 / math.sqrt(2.0 * math.pi))
            d_act = mm_nt(d_res, w2)
            d_hid_f = (d_act * slope).astype(BF)
            gb1_ref[0:1, cols] += jnp.sum(d_hid_f.astype(F32), 0, keepdims=True)
            res = mm(act, w2)
            d_rows = mm_nt(d_hid_f, w1)
            if f == 0:
                xout[...] = res
                dout[...] = d_rows
            else:
                xout[...] += res
                dout[...] += d_rows
            s1[:, cols] += mm_tn(rows_in, d_hid_f)
            s2[cols, :] += mm_tn(act, d_res)
        for j in range(GROUP):
            b = order[g * GROUP + j]
            y_ref[b // mbc, 0, b % mbc] = (
                xout[j * CAP : (j + 1) * CAP, :] + b2_ref[0:1, :]
            ).astype(BF)
            y_ref[b // mbc, 1, b % mbc] = dout[j * CAP : (j + 1) * CAP, :].astype(BF)
        return carry

    lax.fori_loop(0, (live_total + GROUP - 1) // GROUP, one_group, 0)
    if last:
        g1_ref[...] = s1[...].astype(BF)
        g2_ref[...] = s2[...].astype(BF)


def expert_call(m0, mbc, last, counts, x, w1, w2, b1, b2, acc):
    width, ff = w1.shape
    grad_type = BF if last else F32
    vm = pl.BlockSpec(memory_space=pltpu.VMEM)
    scratch = []
    if last:
        scratch += [pltpu.VMEM((width, ff), F32), pltpu.VMEM((ff, width), F32)]
    scratch += [
        pltpu.SMEM((EXPERTS * mbc,), jnp.int32),
        pltpu.VMEM((GROUP * CAP, width), BF),
        pltpu.VMEM((GROUP * CAP, width), BF),
        pltpu.VMEM((GROUP * CAP, width), F32),
        pltpu.VMEM((GROUP * CAP, width), F32),
    ]
    return pl.pallas_call(
        functools.partial(expert_kernel, m0, mbc, acc is not None, last),
        in_specs=[pl.BlockSpec(memory_space=pltpu.SMEM)] + [vm] * (5 + (0 if acc is None else 4)),
        out_specs=[vm] * 5,
        out_shape=[
            jax.ShapeDtypeStruct(x.shape, BF),
            jax.ShapeDtypeStruct((width, ff), grad_type),
            jax.ShapeDtypeStruct((ff, width), grad_type),
            jax.ShapeDtypeStruct((8, ff), F32),
            jax.ShapeDtypeStruct((8, width), F32),
        ],
        scratch_shapes=scratch,
        compiler_params=pltpu.CompilerParams(vmem_limit_bytes=VMEM_LIMIT),
        cost_estimate=pl.CostEstimate(
            flops=mbc * 20 * 10**9, bytes_accessed=mbc * 10 * 10**6, transcendentals=0
        ),
        name="expert_both",
    )(counts, x, w1, w2, b1, b2, *(() if acc is None else acc))


def backward_kernel(
    m0,
    seq_len,
    pad_len,
    has_acc,
    cnt_ref,
    img_ref,
    cot_ref,
    meta_ref,
    y_ref,
    qkv_ref,
    p_ref,
    att_ref,
    mid_ref,
    rp_ref,
    coef_ref,
    w_ref,
    small_ref,
    *rest,
):
    if has_acc:
        accw_ref, accs_ref = rest[:2]
        rest = rest[4:]
    out_ref, grad_ref, gw_ref, gs_ref, xs, cs, dq = rest
    step = pl.program_id(0)
    width = xs.shape[1]
    alive = cnt_ref[0] > 2 * (m0 + step)

    @pl.when(step == 0)
    def _():
        if has_acc:
            gw_ref[...] = accw_ref[...]
            gs_ref[...] = accs_ref[...]
        else:
            gw_ref[...] = jnp.zeros_like(gw_ref)
            gs_ref[...] = jnp.zeros_like(gs_ref)

    @pl.when(jnp.logical_not(alive))
    def _():
        out_ref[...] = jnp.zeros_like(out_ref)
        grad_ref[...] = jnp.zeros_like(grad_ref)

    def add_row(row, value):
        gs_ref[row : row + 1, :] += jnp.sum(value, 0, keepdims=True)

    @pl.when(alive)
    def _():
        load_padded(xs, img_ref, seq_len, pad_len)
        load_padded(cs, cot_ref, seq_len, pad_len)
        rows = xs.shape[0]
        live = meta_ref[0, :, COL_LIVE : COL_LIVE + 1]
        d_final = cs[...] * live
        middle = mid_ref[0]
        rp = rp_ref[0]
        lane = lax.broadcasted_iota(jnp.int32, (1, SMALL), 1)
        lane_f = lane.astype(F32)
        slot = lax.broadcasted_iota(jnp.int32, (1, EXPERTS * CAP), 1).astype(F32)
        res = y_ref[:, 0, 0].reshape(EXPERTS * CAP, width)
        d_rows = y_ref[:, 1, 0].reshape(EXPERTS * CAP, width)
        final = middle
        d_prob = coef_ref[0:1, :] * live
        sel_all = None
        for target, route, kept in ((COL_T0, COL_R0, COL_K0), (COL_T1, COL_R1, COL_K1)):
            sel = jnp.where(slot == meta_ref[0, :, target : target + 1], 1.0, 0.0).astype(BF)
            sel_all = sel if sel_all is None else sel_all + sel
            picked = mm(sel, res)
            keep = meta_ref[0, :, kept : kept + 1]
            hot = lane_f == meta_ref[0, :, route : route + 1]
            gate = jnp.sum(jnp.where(hot, rp, 0.0), -1, keepdims=True) * keep
            final = final + gate * picked
            d_gate = jnp.sum(picked * d_final, -1, keepdims=True) * keep
            d_prob = d_prob + jnp.where(hot, d_gate, 0.0)
        final = final * live
        for i in range(2):
            out_ref[i] = final[i * pad_len : i * pad_len + seq_len, :].astype(BF)
        d_mixed = mm(sel_all, d_rows)
        d_logits = (rp * (d_prob - jnp.sum(rp * d_prob, -1, keepdims=True))).astype(BF)
        d_mixed = d_mixed + mm_nt(d_logits, w_ref[:, 4 * width : 4 * width + SMALL])
        gain2 = small_ref[ROW_GAIN2 : ROW_GAIN2 + 1, :]
        xhat2, inv2 = norm_parts(middle)
        mixed = (xhat2 * gain2 + small_ref[ROW_BIAS2 : ROW_BIAS2 + 1, :]).astype(BF)
        gs_ref[0:EXPERTS, :] += mm_tn(d_logits, mixed)[0:EXPERTS, :]
        add_row(ROW_GAIN2, d_mixed * xhat2)
        add_row(ROW_BIAS2, d_mixed)
        d_middle = d_final + norm_back(d_mixed, xhat2, inv2, gain2)
        add_row(ROW_OBIAS, d_middle)
        cs[...] = d_middle
        d_branch = d_middle.astype(BF)
        gw_ref[:, 3 * width : 4 * width] += mm_tn(att_ref[0], d_branch)
        d_att_all = mm_nt(d_branch, w_ref[:, 3 * width : 4 * width]).astype(BF)
        low, high, low_mask = half_masks()
        scale = HEAD_DIM**-0.5
        for i in range(2):
            span = slice(i * pad_len, (i + 1) * pad_len)
            for hp in range(HEADS // 2):
                at = hp * PAIR
                q = qkv_ref[0, span, at : at + PAIR]
                k = qkv_ref[0, span, width + at : width + at + PAIR]
                v = qkv_ref[0, span, 2 * width + at : 2 * width + at + PAIR]
                d_att = stack_heads(d_att_all[span, at : at + PAIR], low, high)
                p = p_ref[0, i, hp]
                pf = p.astype(F32)
                d_attn = mm_nt(d_att, v)
                d_s = (pf * (d_attn - jnp.sum(pf * d_attn, -1, keepdims=True))).astype(BF)
                d_v = mm_tn(p, d_att)
                d_k = mm_tn(d_s, stack_heads(q, low, high)) * scale
                d_q = mm(d_s, k) * scale
                dq[span, at : at + PAIR] = jnp.where(
                    low_mask, d_q[:pad_len], d_q[pad_len:]
                ).astype(BF)
                dq[span, width + at : width + at + PAIR] = d_k.astype(BF)
                dq[span, 2 * width + at : 2 * width + at + PAIR] = d_v.astype(BF)
        gain1 = small_ref[ROW_GAIN1 : ROW_GAIN1 + 1, :]
        xhat, inv = norm_parts(xs[...])
        normed = (xhat * gain1 + small_ref[ROW_BIAS1 : ROW_BIAS1 + 1, :]).astype(BF)
        add_row(ROW_QBIAS, dq[:, 0:width].astype(F32))
        add_row(ROW_VBIAS, dq[:, 2 * width : 3 * width].astype(F32))
        gw_ref[:, 0 : 3 * width] += mm_tn(normed, dq[...])
        d_normed = mm_nt(dq[...], w_ref[:, 0 : 3 * width])
        add_row(ROW_GAIN1, d_normed * xhat)
        add_row(ROW_BIAS1, d_normed)
        d_tok = cs[...] + norm_back(d_normed, xhat, inv, gain1)
        for i in range(2):
            grad_ref[i] = d_tok[i * pad_len : i * pad_len + seq_len, :].astype(BF)


def backward_call(m0, mbc, images, cotangent, count, meta, back, saved, coef, weights, small, acc):
    seq_len, width = images.shape[1], images.shape[2]
    rows = meta.shape[1]
    pad_len = rows // 2
    mb = images.shape[0] // MICRO
    qkv, probs, att, mid, rp = saved
    at = lambda i: i + m0
    image_block = pl.BlockSpec((mb, seq_len, width), lambda i: (at(i), 0, 0))
    in_specs = [
        pl.BlockSpec(memory_space=pltpu.SMEM),
        image_block,
        image_block,
        pl.BlockSpec((1, rows, 8), lambda i: (at(i), 0, 0)),
        pl.BlockSpec((EXPERTS, 2, 1, CAP, width), lambda i: (0, 0, i, 0, 0)),
        pl.BlockSpec((1, rows, 3 * width), lambda i: (i, 0, 0)),
        pl.BlockSpec((1, 2, HEADS // 2, rows, pad_len), lambda i: (i, 0, 0, 0, 0)),
        pl.BlockSpec((1, rows, width), lambda i: (i, 0, 0)),
        pl.BlockSpec((1, rows, width), lambda i: (i, 0, 0)),
        pl.BlockSpec((1, rows, SMALL), lambda i: (i, 0, 0)),
        full_block(coef.shape),
        full_block(weights.shape),
        full_block(small.shape),
    ]
    args = [count, images, cotangent, meta, back, qkv, probs, att, mid, rp, coef, weights, small]
    aliases = {}
    if acc is not None:
        base = len(args)
        in_specs += [full_block(acc[0].shape), full_block(acc[1].shape)]
        in_specs += [pl.BlockSpec(memory_space=pl.ANY)] * 2
        args += list(acc)
        aliases = {base + 2: 0, base + 3: 1}
    return pl.pallas_call(
        functools.partial(backward_kernel, m0, seq_len, pad_len, acc is not None),
        grid=(mbc,),
        in_specs=in_specs,
        out_specs=[
            image_block,
            image_block,
            full_block((width, 4 * width)),
            full_block((GRAD_ROWS, width)),
        ],
        out_shape=[
            jax.ShapeDtypeStruct(images.shape, BF),
            jax.ShapeDtypeStruct(images.shape, BF),
            jax.ShapeDtypeStruct((width, 4 * width), F32),
            jax.ShapeDtypeStruct((GRAD_ROWS, width), F32),
        ],
        scratch_shapes=[
            pltpu.VMEM((rows, width), F32),
            pltpu.VMEM((rows, width), F32),
            pltpu.VMEM((rows, 3 * width), BF),
        ],
        input_output_aliases=aliases,
        compiler_params=pltpu.CompilerParams(vmem_limit_bytes=VMEM_LIMIT),
        cost_estimate=pl.CostEstimate(
            flops=mbc * 20 * 10**9, bytes_accessed=mbc * 10 * 10**6, transcendentals=0
        ),
        name="dense_backward",
    )(*args)


def shards(
    total,
    images,
    image_count,
    expert_index,
    expert_slot,
    keep,
    cotangent,
    ln1_gain,
    ln1_bias,
    qkv_weight,
    qv_bias,
    out_weight,
    out_bias,
    ln2_gain,
    ln2_bias,
    router_weight,
    expert_in,
    expert_in_bias,
    expert_out,
    expert_out_bias,
):
    slots, seq_len, width = images.shape
    planes = total // EXPERTS
    rows = width // total
    ff = expert_in.shape[2]
    ff_rows = ff // total
    mb = slots // MICRO
    pad_len = -(-seq_len // 16) * 16
    plane_groups = [[z * EXPERTS + p for p in range(EXPERTS)] for z in range(planes)]
    z_groups = [[z * EXPERTS + p for z in range(planes)] for p in range(EXPERTS)]

    def plane_swap(v):
        return lax.all_to_all(v, "dp", 0, 0, tiled=True, axis_index_groups=plane_groups)

    def z_swap(v):
        return lax.all_to_all(v, "dp", 0, 0, tiled=True, axis_index_groups=z_groups)

    def z_gather(v):
        return lax.all_gather(v, "dp", axis=0, tiled=True, axis_index_groups=z_groups)

    small_cols = jnp.concatenate(
        [
            router_weight,
            ln1_gain[:, None],
            ln1_bias[:, None],
            qv_bias.T,
            out_bias[:, None],
            ln2_gain[:, None],
            ln2_bias[:, None],
            jnp.zeros((rows, SMALL - 15), BF),
        ],
        1,
    )
    packed = jnp.concatenate([qkv_weight, out_weight, small_cols], 1)
    wide = packed.shape[1]
    packed = z_gather(packed)
    packed = plane_swap(jnp.broadcast_to(packed[None], (EXPERTS,) + packed.shape))
    weights = (
        packed.reshape(EXPERTS, planes, rows, wide).transpose(1, 0, 2, 3).reshape(width, wide)
    )
    small = weights[:, 4 * width :].astype(F32).T

    live_img = jnp.arange(slots) < image_count[0]
    live_tok = jnp.broadcast_to(live_img[:, None, None], (slots, seq_len, 1)).astype(F32)
    target = jnp.where(keep == 1, expert_index * CAP + expert_slot, -1).astype(F32)
    hits = (expert_index[..., None] == jnp.arange(EXPERTS)).astype(F32) * live_tok[..., None]
    local_counts = jnp.sum(hits, axis=(0, 1, 2))
    meta = jnp.concatenate(
        [
            target,
            expert_index.astype(F32),
            keep.astype(F32),
            live_tok,
            jnp.zeros((slots, seq_len, 1), F32),
        ],
        -1,
    )
    fill = jnp.array([-1.0, -1.0, 0.0, 0.0, 0.0, 0.0, 0.0, 0.0], F32)
    meta = jnp.concatenate(
        [meta, jnp.broadcast_to(fill, (slots, pad_len - seq_len, 8))], 1
    ).reshape(MICRO, mb * pad_len, 8)
    lane_t = meta.transpose(0, 2, 1)

    high = jnp.floor(local_counts * (1.0 / 128.0))
    told = jnp.concatenate(
        [
            expert_in_bias,
            expert_out_bias,
            jnp.broadcast_to(
                jnp.concatenate(
                    [high, local_counts - 128.0 * high, image_count.astype(F32)]
                ).astype(BF)[None],
                (EXPERTS, 2 * EXPERTS + 1),
            ),
        ],
        1,
    )
    told = jnp.pad(told, ((0, 0), (0, 128 - told.shape[1])))
    told = jnp.broadcast_to(told[None], (planes,) + told.shape).reshape(total, 128)
    heard = lax.all_to_all(told, "dp", 0, 0, tiled=True).astype(F32)
    in_bias = heard[:, :ff_rows].reshape(1, ff)
    out_bias_e = heard[:, ff_rows : ff_rows + rows].reshape(1, width)
    base = ff_rows + rows
    tail = heard[:, base : base + 2 * EXPERTS + 1]
    counts_all = jnp.sum(tail[:, :EXPERTS] * 128.0 + tail[:, EXPERTS : 2 * EXPERTS], 0)
    all_images = tail[:, 2 * EXPERTS]
    live_total = jnp.sum(all_images) * float(seq_len)
    plane_id = lax.axis_index("dp") // EXPERTS
    plane_counts = lax.dynamic_slice(all_images, (plane_id * EXPERTS,), (EXPERTS,)).astype(
        jnp.int32
    )
    coef = jnp.pad(BALANCE_WEIGHT * EXPERTS * counts_all / live_total, (0, SMALL - EXPERTS))
    coef = jnp.broadcast_to(coef[None], (8, SMALL))
    in_bias = jnp.broadcast_to(in_bias, (8, ff))
    out_bias_e = jnp.broadcast_to(out_bias_e, (8, width))

    w1 = z_gather(plane_swap(expert_in).reshape(EXPERTS * rows, ff))
    w2 = z_gather(plane_swap(expert_out).reshape(EXPERTS * ff_rows, width))

    chunks = 2
    mbc = MICRO // chunks
    saved, sent, prob_sums = [], [], []
    for c in range(chunks):
        xd, qkv, probs, att, mid, rp, prob = forward_call(
            c * mbc, mbc, images, cotangent, image_count, lane_t, meta, weights, small
        )
        saved.append((qkv, probs, att, mid, rp))
        prob_sums.append(prob[0, :EXPERTS])
        sent.append(plane_swap(xd))
    acc = None
    back = []
    for c in range(chunks):
        y, *acc = expert_call(
            c * mbc, mbc, c == chunks - 1, plane_counts, sent[c], w1, w2, in_bias, out_bias_e, acc
        )
        back.append(plane_swap(y))
    g1, g2, gb1, gb2 = acc

    def z_reduce(v):
        return lax.psum_scatter(
            v, "dp", scatter_dimension=0, tiled=True, axis_index_groups=z_groups
        )

    expert_in_grad = plane_swap(z_reduce(g1).reshape(EXPERTS, rows, ff)).astype(F32)
    expert_out_grad = plane_swap(z_reduce(g2).reshape(EXPERTS, ff_rows, width)).astype(F32)
    bias_told = jnp.concatenate([gb1[0].reshape(total, ff_rows), gb2[0].reshape(total, rows)], 1)
    bias_told = jnp.pad(bias_told, ((0, 0), (0, 128 - bias_told.shape[1])))
    bias_heard = lax.all_to_all(bias_told, "dp", 0, 0, tiled=True)
    bias_heard = jnp.sum(bias_heard.reshape(planes, EXPERTS, 128), 0)
    expert_in_bias_grad = bias_heard[:, :ff_rows]
    expert_out_bias_grad = bias_heard[:, ff_rows : ff_rows + rows]

    acc = None
    for c in range(chunks):
        block_out, image_grad, gw, gs = backward_call(
            c * mbc,
            mbc,
            images,
            cotangent,
            image_count,
            meta,
            back[c],
            saved[c],
            coef,
            weights,
            small,
            acc,
        )
        acc = (gw, gs, block_out, image_grad)

    prob_sum = prob_sums[0]
    for piece in prob_sums[1:]:
        prob_sum = prob_sum + piece
    p_hi = prob_sum.astype(BF)
    p_mid = (prob_sum - p_hi.astype(F32)).astype(BF)
    extra = jnp.broadcast_to(jnp.concatenate([p_hi, p_mid])[None], (width, 2 * EXPERTS))
    grads = jnp.concatenate(
        [
            gw.astype(BF),
            gs.T.astype(BF),
            extra,
            jnp.zeros((width, SMALL - GRAD_ROWS - 2 * EXPERTS), BF),
        ],
        1,
    )
    grads = grads.reshape(planes, EXPERTS, rows, wide).transpose(1, 0, 2, 3)
    grads = plane_swap(grads.reshape(EXPERTS, planes * rows, wide))
    grads = jnp.sum(grads.astype(F32), 0).reshape(planes, rows, wide)
    grads = jnp.sum(z_swap(grads), 0)
    small_grads = grads[:, 4 * width :]
    prob_all = (
        small_grads[0, GRAD_ROWS : GRAD_ROWS + EXPERTS]
        + small_grads[0, GRAD_ROWS + EXPERTS : GRAD_ROWS + 2 * EXPERTS]
    )
    balance = EXPERTS * jnp.sum(counts_all / live_total * prob_all / live_total)
    return (
        block_out,
        image_grad,
        balance,
        small_grads[:, ROW_GAIN1],
        small_grads[:, ROW_BIAS1],
        grads[:, : 3 * width],
        small_grads[:, ROW_QBIAS : ROW_VBIAS + 1].T,
        grads[:, 3 * width : 4 * width],
        small_grads[:, ROW_OBIAS],
        small_grads[:, ROW_GAIN2],
        small_grads[:, ROW_BIAS2],
        small_grads[:, :EXPERTS],
        expert_in_grad,
        expert_in_bias_grad,
        expert_out_grad,
        expert_out_bias_grad,
    )


def solution(mesh):
    placed = (
        P("dp", None, None),
        P("dp"),
        P("dp", None, None),
        P("dp", None, None),
        P("dp", None, None),
        P("dp", None, None),
        P("dp"),
        P("dp"),
        P("dp", None),
        P(None, "dp"),
        P("dp", None),
        P("dp"),
        P("dp"),
        P("dp"),
        P("dp", None),
        P(None, "dp", None),
        P(None, "dp"),
        P(None, "dp", None),
        P(None, "dp"),
    )
    return jax.shard_map(
        functools.partial(shards, mesh.shape["dp"]),
        mesh=mesh,
        in_specs=placed,
        out_specs=(
            P("dp", None, None),
            P("dp", None, None),
            P(),
            P("dp"),
            P("dp"),
            P("dp", None),
            P(None, "dp"),
            P("dp", None),
            P("dp"),
            P("dp"),
            P("dp"),
            P("dp", None),
            P(None, "dp", None),
            P(None, "dp"),
            P(None, "dp", None),
            P(None, "dp"),
        ),
        check_vma=False,
    )
```

time: 2570 us -> 484 us (0.19)
  waiting for transfers between devices: 1110 us -> 179 us
  matrix products: 568 us -> 0 us
  local copies, waits for them, and re-layouts: 377 us -> 35.2 us
  blocking collectives: 314 us -> 40.8 us
  other arithmetic: 164 us -> 12.8 us
  Pallas kernels: 0 us -> 123 us
  starting transfers between devices: 0.62 us -> 66.3 us
    reduce_scatter x4 -> x2, waiting for transfers between devices: 958 us -> 0.01 us  [z_reduce(): lax.psum_scatter(v, 'dp', scatter_dimension=0, tiled=True, axis_index_gro...]
    dot_general x80 -> x0, matrix products: 549 us -> none  [the longest x4 130 us: backward_pass(): jnp.einsum('ecd,efd->ecf', d_res_low, outer_mat, preferred_element_type=j...]
    all_gather x5 -> x1, blocking collectives: 194 us -> 14.4 us  [z_gather(): lax.all_gather(v, 'dp', axis=0, tiled=True, axis_index_groups=z_groups)]
    all_to_all x0 -> x12, waiting for transfers between devices: none -> 179 us  [the longest x10 169 us: plane_swap(): lax.all_to_all(v, 'dp', 0, 0, tiled=True, axis_index_groups=plane_groups)]
    unnamed x15 -> x4, waiting for transfers between devices: 154 us -> 0.28 us
    pallas_call x0 -> x6, Pallas kernels: none -> 123 us  [the longest x2 63.1 us: expert_call(): pl.pallas_call(functools.partial(expert_kernel, m0, mbc, acc is not None,...]
    reshape x64 -> x1, local copies, waits for them, and re-layouts: 106 us -> 1.55 us  [shards(): grads = grads.reshape(planes, EXPERTS, rows, wide).transpose(1, 0, 2, 3)]
    gather x36 -> x0, local copies, waits for them, and re-layouts: 89.9 us -> none  [the longest x20 39.4 us: forward_pass(): jnp.take_along_axis(router_prob, routes, axis=1)]
  transfers between devices with their start and end apart: 11 -> 16, of which waited for: 6 -> 9; matrix products, arithmetic and copies ran while one was open for 43% -> 8% of each run, Pallas kernels for 0% -> 22%
where the time goes in v1:
time: 484 us; the launch traced here: 475 us
  waiting for transfers between devices  179 us (37%)
  Pallas kernels  123 us (25%)
  starting transfers between devices  66.3 us (14%)
  blocking collectives  40.8 us (8%)
  local copies, waits for them, and re-layouts  35.2 us (7%)
  between operations  17.4 us (4%)
  other arithmetic  12.8 us (3%)
    all_to_all x10, waiting for transfers between devices, plane_swap(): lax.all_to_all(v, 'dp', 0, 0, tiled=True, axis_index_groups=plane_groups)  169 us
    pallas_call x2, Pallas kernels, expert_call(): pl.pallas_call(functools.partial(expert_kernel, m0, mbc, acc is not None,...  63.1 us
    all_to_all x10, starting transfers between devices, plane_swap(): lax.all_to_all(v, 'dp', 0, 0, tiled=True, axis_index_groups=plane_groups)  50.6 us
    pallas_call x2, Pallas kernels, backward_call(): pl.pallas_call(functools.partial(backward_kernel, m0, seq_len, pad_len, a...  35.8 us
    all_to_all x1, blocking collectives, shards(): bias_heard = lax.all_to_all(bias_told, 'dp', 0, 0, tiled=True)  26.5 us
    pallas_call x2, Pallas kernels, forward_call(): pl.pallas_call(functools.partial(forward_kernel, m0, seq_len, pad_len), g...  24.5 us
    all_gather x1, blocking collectives, z_gather(): lax.all_gather(v, 'dp', axis=0, tiled=True, axis_index_groups=z_groups)  14.4 us
    unnamed x34, local copies, waits for them, and re-layouts  14.1 us
  transfers between devices with their start and end apart: 16, of which 9 were waited for; matrix products, arithmetic and copies ran while one was open for 8% of the time, Pallas kernels for 22%

profile of v1, /device:TPU:0, one launch (start us, length us, event | category | flops | bytes accessed | tf_op | source)
XLA Modules:
  0.0 475.3 jit_solution(16323003483574728414)
XLA Ops:
  7.2 5.2 %all-to-all-start.3 = ((bf16[8,16,2048]{2,1,0:T(8,128)(2,1)}), bf16[8,16,2048]{2,1,0:T(8,128)(2,1)S(1)}, u32[]{:S(2)}, u32[]{:S(2)}) async-start(bf16[8,16,2048]{2,1,0:T(8,128)(2,1)} %param.35), calls=%async_computation.3 | async-start | bytes 1048576 | tf_op jit(solution)/shard_map/all_to_all | solution.py:590
  18.5 14.4 %all_gather.9 = bf16[64,2176]{1,0:T(8,128)(2,1)S(1)} all-gather(bf16[16,2176]{1,0:T(8,128)(2,1)S(1)} %concatenate.33), channel_id=1, replica_groups={{0,8,16,24},{1,9,17,25},{2,10,18,26},{3,11,19,27},{4,12,20,28},{5,13,21..., dimensions={0}, use_global_device_ids=true | all-gather | bytes 348160 | tf_op jit(solution)/shard_map/all_gather | solution.py:596
  34.5 4.0 all-to-all-start.1
  42.0 3.2 copy.195.img_ref
  46.9 19.7 %all-to-all-done.1 = bf16[8,64,2176]{2,1,0:T(8,128)(2,1)S(1)} async-done(((bf16[8,64,2176]{2,1,0:T(8,128)(2,1)}), bf16[8,64,2176]{2,1,0:T(8,128)(2,1)S(1)}, u32[]{:S(2)}, u32[]{:S(2)}) %all-to-all-start.1) | async-done | bytes 2228256 | tf_op jit(solution)/shard_map/all_to_all | solution.py:590
  66.6 4.4 all-to-all-start
  73.5 4.8 %all-to-all-done = bf16[32,1,128]{2,1,0:T(2,128)(2,1)S(1)} async-done(((bf16[32,1,128]{2,1,0:T(2,128)(2,1)}), bf16[32,1,128]{2,1,0:T(2,128)(2,1)S(1)}, u32[]{:S(2)}, u32[]{:S(2)}) %all-to-all-start) | async-done | bytes 8224 | tf_op jit(solution)/shard_map/all_to_all | solution.py:657
  78.3 3.5 all-to-all-start.4
  81.8 17.5 %dense_forward.3 = (bf16[8,2,2,128,512]{4,3,2,1,0:T(8,128)(2,1)}, bf16[2,416,1536]{2,1,0:T(8,128)(2,1)}, bf16[2,2,4,416,208]{4,3,2,1,0:T(8,128)(2,1)}, bf16[2,41...) custom-call(s32[1]{0:T(128)} %copy.206.cnt_ref, ...), custom_call_target="tpu_custom_call" | custom-call | flops 24000000000 | bytes 20000000 | tf_op jit(solution)/shard_map/dense_forward/pallas_call | solution.py:190
  100.2 4.6 all-to-all-start.5
  107.0 7.0 %dense_forward.2 = (bf16[8,2,2,128,512]{4,3,2,1,0:T(8,128)(2,1)}, bf16[2,416,1536]{2,1,0:T(8,128)(2,1)}, bf16[2,2,4,416,208]{4,3,2,1,0:T(8,128)(2,1)}, bf16[2,41...) custom-call(s32[1]{0:T(128)} %copy.206.cnt_ref, ...), custom_call_target="tpu_custom_call" | custom-call | flops 24000000000 | bytes 20000000 | tf_op jit(solution)/shard_map/dense_forward/pallas_call | solution.py:190
  114.0 39.8 %all-to-all-done.5.x_ref = bf16[8,2,2,128,512]{4,3,2,1,0:T(8,128)(2,1)} async-done(((bf16[8,2,2,128,512]{4,3,2,1,0:T(8,128)(2,1)}), bf16[8,2,2,128,512]{4,3,2,1,0:T(8,128)(2,1)}, u32[]{:S(2)}, u32[]{:S(2)}) %all-to-all-start.5) | async-done | bytes 4194336 | tf_op jit(solution)/shard_map/all_to_all | solution.py:590
  153.8 4.6 all-to-all-start.2
  159.8 44.3 %expert_both.2 = (bf16[8,2,2,128,512]{4,3,2,1,0:T(8,128)(2,1)}, f32[512,2048]{1,0:T(8,128)}, f32[2048,512]{1,0:T(8,128)}, f32[8,2048]{1,0:T(8,128)}, f32[8,512]{1,0:T(8,128)}) custom-call(s32[8]{0:T(128)} %convert_reduce_fusion.1.cnt_ref, bf16[8,2,2,128,512]{4,3,2,1,0:T(8,128)(2,1)} %all-to-all-done.5.x_ref, ...), custom_call_target="tpu_custom_call" | custom-call | flops 40000000000 | bytes 20000000 | tf_op jit(solution)/shard_map/expert_both/pallas_call | solution.py:350
  204.1 3.5 all-to-all-done.2.x_ref
  207.6 18.8 %expert_both.3 = (bf16[8,2,2,128,512]{4,3,2,1,0:T(8,128)(2,1)}, bf16[512,2048]{1,0:T(8,128)(2,1)}, bf16[2048,512]{1,0:T(8,128)(2,1)}, f32[8,2048]{1,0:T(8,128)}, f32[8,512]{1,0:T(8,128)}) custom-call(s32[8]{0:T(128)} %convert_reduce_fusion.1.cnt_ref, bf16[8,2,2,128,512]{4,3,2,1,0:T(8,128)(2,1)} %all-to-all-done.2.x_ref, ...), custom_call_target="tpu_custom_call" | custom-call | flops 40000000000 | bytes 20000000 | tf_op jit(solution)/shard_map/expert_both/pallas_call | solution.py:350
  228.2 26.5 %all_to_all.73 = f32[32,1,128]{2,1,0:T(1,128)S(1)} all-to-all(f32[32,1,128]{2,1,0:T(1,128)S(1)} %bitcast.73), channel_id=1, replica_groups=mesh['dp'=32] {'dp'}, dimensions={0} | all-to-all | bytes 32768 | tf_op jit(solution)/shard_map/all_to_all | solution.py:705
  254.7 4.6 all-to-all-start.7
  261.6 46.8 %all-to-all-done.7.y_ref = bf16[8,2,2,128,512]{4,3,2,1,0:T(8,128)(2,1)} async-done(((bf16[8,2,2,128,512]{4,3,2,1,0:T(8,128)(2,1)}), bf16[8,2,2,128,512]{4,3,2,1,0:T(8,128)(2,1)}, u32[]{:S(2)}, u32[]{:S(2)}) %all-to-all-start.7) | async-done | bytes 4194336 | tf_op jit(solution)/shard_map/all_to_all | solution.py:590
  308.4 5.0 %all-to-all-start.6 = ((bf16[8,2,2,128,512]{4,3,2,1,0:T(8,128)(2,1)}), bf16[8,2,2,128,512]{4,3,2,1,0:T(8,128)(2,1)}, u32[]{:S(2)}, u32[]{:S(2)}) async-start(bf16[8,2,2,128,512]{4,3,2,1,0:T(8,128)(2,1)} %get-tuple-element.54), calls=%async_computation.6 | async-start | bytes 8388608 | tf_op jit(solution)/shard_map/all_to_all | solution.py:590
  314.0 25.9 %dense_backward.2 = (bf16[8,197,512]{2,1,0:T(8,128)(2,1)}, bf16[8,197,512]{2,1,0:T(8,128)(2,1)}, f32[512,2048]{1,0:T(8,128)}, f32[16,512]{1,0:T(8,128)}) custom-call(s32[1]{0:T(128)} %copy.206.cnt_ref, bf16[8,197,512]{2,1,0:T(8,128)(2,1)} %copy.195.img_ref, bf16[8,197,512]{2,1,0:T(8,128)(2,1)} %copy.196.cot_ref, f32[4,416,8]{2,1,0:T(8,128)} %bitcast.58, ...), custom_call_target="tpu_custom_call" | custom-call | flops 40000000000 | bytes 20000000 | tf_op jit(solution)/shard_map/dense_backward/pallas_call | solution.py:527
  339.9 22.6 %all-to-all-done.6.y_ref = bf16[8,2,2,128,512]{4,3,2,1,0:T(8,128)(2,1)} async-done(((bf16[8,2,2,128,512]{4,3,2,1,0:T(8,128)(2,1)}), bf16[8,2,2,128,512]{4,3,2,1,0:T(8,128)(2,1)}, u32[]{:S(2)}, u32[]{:S(2)}) %all-to-all-start.6) | async-done | bytes 4194336 | tf_op jit(solution)/shard_map/all_to_all | solution.py:590
  362.5 3.7 all-to-all-start.12
  366.2 9.9 %dense_backward.3 = (bf16[8,197,512]{2,1,0:T(8,128)(2,1)}, bf16[8,197,512]{2,1,0:T(8,128)(2,1)}, f32[512,2048]{1,0:T(8,128)}, f32[16,512]{1,0:T(8,128)}) custom-call(s32[1]{0:T(128)} %copy.206.cnt_ref, bf16[8,197,512]{2,1,0:T(8,128)(2,1)} %copy.195.img_ref, bf16[8,197,512]{2,1,0:T(8,128)(2,1)} %copy.196.cot_ref, ...), custom_call_target="tpu_custom_call", output_to_operand_aliasing={{0}: (15, {}), {1}: (16, {})} | custom-call | flops 40000000000 | bytes 20000000 | tf_op jit(solution)/shard_map/dense_backward/pallas_call | solution.py:527
  376.9 3.8 convert_element_type.79
  380.8 3.6 concatenate.35
  386.0 12.0 %all-to-all-start.8 = ((bf16[8,64,2176]{2,1,0:T(8,128)(2,1)}), bf16[8,64,2176]{2,1,0:T(8,128)(2,1)S(1)}, u32[]{:S(2)}, u32[]{:S(2)}) async-start(bf16[8,64,2176]{2,1,0:T(8,128)(2,1)} %bitcast.53), calls=%async_computation.8 | async-start | bytes 4456448 | tf_op jit(solution)/shard_map/all_to_all | solution.py:590
  398.0 28.0 %all-to-all-done.8 = bf16[8,64,2176]{2,1,0:T(8,128)(2,1)S(1)} async-done(((bf16[8,64,2176]{2,1,0:T(8,128)(2,1)}), bf16[8,64,2176]{2,1,0:T(8,128)(2,1)S(1)}, u32[]{:S(2)}, u32[]{:S(2)}) %all-to-all-start.8) | async-done | bytes 2228256 | tf_op jit(solution)/shard_map/all_to_all | solution.py:590
  426.0 3.5 all-to-all-start.10
  430.6 8.6 %all-to-all-done.10 = bf16[8,16,2048]{2,1,0:T(8,128)(2,1)S(1)} async-done(((bf16[8,16,2048]{2,1,0:T(8,128)(2,1)}), bf16[8,16,2048]{2,1,0:T(8,128)(2,1)S(1)}, u32[]{:S(2)}, u32[]{:S(2)}) %all-to-all-start.10) | async-done | bytes 524320 | tf_op jit(solution)/shard_map/all_to_all | solution.py:590
  439.2 10.7 %all-to-all-start.9 = ((f32[4,16,2176]{2,1,0:T(8,128)}), f32[4,16,2176]{2,1,0:T(8,128)S(1)}, u32[]{:S(2)}, u32[]{:S(2)}) async-start(f32[4,16,2176]{2,1,0:T(8,128)} %bitcast.22), calls=%async_computation.9 | async-start | bytes 1114112 | tf_op jit(solution)/shard_map/all_to_all | solution.py:593
  457.5 5.2 %all-to-all-done.9 = f32[4,16,2176]{2,1,0:T(8,128)S(1)} async-done(((f32[4,16,2176]{2,1,0:T(8,128)}), f32[4,16,2176]{2,1,0:T(8,128)S(1)}, u32[]{:S(2)}, u32[]{:S(2)}) %all-to-all-start.9) | async-done | bytes 557088 | tf_op jit(solution)/shard_map/all_to_all | solution.py:593
  (113 shorter events, 38.3 us)
Async XLA Ops:
  7.2 25.7 %all-to-all-start.3 = ((bf16[8,16,2048]{2,1,0:T(8,128)(2,1)}), bf16[8,16,2048]{2,1,0:T(8,128)(2,1)S(1)}, u32[]{:S(2)}, u32[]{:S(2)}) async-start(bf16[8,16,2048]{2,1,0:T(8,128)(2,1)} %param.35), calls=%async_computation.3 | async-start | bytes 1048576 | tf_op jit(solution)/shard_map/all_to_all | solution.py:590
  32.9 1.7 copy-start.2
  34.5 4.8 %copy-start.6 = (s32[8,197,2]{1,2,0:T(2,128)S(1)}, s32[8,197,2]{1,2,0:T(2,128)}, u32[]{:S(2)}) copy-start(s32[8,197,2]{1,2,0:T(2,128)} %param.22) | copy-start | bytes 37828
  34.5 5.1 %copy-start.10 = (bf16[8,16]{1,0:T(8,128)(2,1)S(1)}, bf16[8,16]{1,0:T(8,128)(2,1)}, u32[]{:S(2)}) copy-start(bf16[8,16]{1,0:T(8,128)(2,1)} %param.38) | copy-start | bytes 772
  34.5 5.1 %copy-start.11 = (bf16[8,64]{1,0:T(8,128)(2,1)S(1)}, bf16[8,64]{1,0:T(8,128)(2,1)}, u32[]{:S(2)}) copy-start(bf16[8,64]{1,0:T(8,128)(2,1)} %param.36) | copy-start | bytes 3076
  34.5 5.2 %copy-start.8 = (s32[8,197,2]{1,2,0:T(2,128)S(1)}, s32[8,197,2]{1,2,0:T(2,128)}, u32[]{:S(2)}) copy-start(s32[8,197,2]{1,2,0:T(2,128)} %param.24) | copy-start | bytes 37828
  34.5 5.2 %copy-start.9 = (s32[8,197,2]{1,2,0:T(2,128)S(1)}, s32[8,197,2]{1,2,0:T(2,128)}, u32[]{:S(2)}) copy-start(s32[8,197,2]{1,2,0:T(2,128)} %param.23) | copy-start | bytes 37828
  34.5 6.1 %copy-start.12 = (f32[8]{0:T(128)S(1)}, f32[8]{0:T(128)}, u32[]{:S(2)}) copy-start(f32[8]{0:T(128)} %constant.51.clone) | copy-start | bytes 100
  34.5 32.1 %all-to-all-start.1 = ((bf16[8,64,2176]{2,1,0:T(8,128)(2,1)}), bf16[8,64,2176]{2,1,0:T(8,128)(2,1)S(1)}, u32[]{:S(2)}, u32[]{:S(2)}) async-start(bf16[8,64,2176]{2,1,0:T(8,128)(2,1)} %broadcast_in_dim.96), calls=%async_computation.1 | async-start | bytes 4456448 | tf_op jit(solution)/shard_map/all_to_all | solution.py:590
  38.6 119.9 %all-gather.3.cloned.1.call-start = ((), (), s32[]{:S(2)}) async-start(), calls=%async_computation.15 | async-start | bytes 2621440 | tf_op jit(solution)/shard_map/all_gather | solution.py:596
  41.0 5.9 %copy-start = (f32[8,208,8]{2,1,0:T(8,128)}, f32[8,208,8]{2,1,0:T(8,128)S(1)}, u32[]{:S(2)}) copy-start(f32[8,208,8]{2,1,0:T(8,128)S(1)} %copy.176) | copy-start | bytes 159748
  42.0 3.2 copy-start.5
  66.6 11.6 %all-to-all-start = ((bf16[32,1,128]{2,1,0:T(2,128)(2,1)}), bf16[32,1,128]{2,1,0:T(2,128)(2,1)S(1)}, u32[]{:S(2)}, u32[]{:S(2)}) async-start(bf16[32,1,128]{2,1,0:T(2,128)(2,1)} %copy.177), calls=%async_computation | async-start | bytes 32768 | tf_op jit(solution)/shard_map/all_to_all | solution.py:657
  71.3 1.3 copy-start.1
  78.3 21.0 %all-to-all-start.4 = ((bf16[8,64,512]{2,1,0:T(8,128)(2,1)}), bf16[8,64,512]{2,1,0:T(8,128)(2,1)S(1)}, u32[]{:S(2)}, u32[]{:S(2)}) async-start(bf16[8,64,512]{2,1,0:T(8,128)(2,1)} %param.37), calls=%async_computation.4 | async-start | bytes 1048576 | tf_op jit(solution)/shard_map/all_to_all | solution.py:590
  99.3 0.8 copy-start.3
  100.2 53.7 %all-to-all-start.5 = ((bf16[8,2,2,128,512]{4,3,2,1,0:T(8,128)(2,1)}), bf16[8,2,2,128,512]{4,3,2,1,0:T(8,128)(2,1)}, u32[]{:S(2)}, u32[]{:S(2)}) async-start(bf16[8,2,2,128,512]{4,3,2,1,0:T(8,128)(2,1)} %get-tuple-element.49), calls=%async_computation.5 | async-start | bytes 8388608 | tf_op jit(solution)/shard_map/all_to_all | solution.py:590
  104.7 53.8 %all-gather.5.cloned.1.call-start = ((), (), s32[]{:S(2)}) async-start(), calls=%async_computation.16 | async-start | bytes 2621440 | tf_op jit(solution)/shard_map/all_gather | solution.py:596
  153.8 53.7 %all-to-all-start.2 = ((bf16[8,2,2,128,512]{4,3,2,1,0:T(8,128)(2,1)}), bf16[8,2,2,128,512]{4,3,2,1,0:T(8,128)(2,1)}, u32[]{:S(2)}, u32[]{:S(2)}) async-start(bf16[8,2,2,128,512]{4,3,2,1,0:T(8,128)(2,1)} %get-tuple-element.48), calls=%async_computation.2 | async-start | bytes 8388608 | tf_op jit(solution)/shard_map/all_to_all | solution.py:590
  158.4 204.1 %reduce-scatter.5.cloned.1.call-start = ((), (), s32[]{:S(2)}) async-start(), calls=%async_computation.18 | async-start | bytes 2621440 | tf_op jit(solution)/shard_map/reduce_scatter | solution.py:697
  254.7 53.7 %all-to-all-start.7 = ((bf16[8,2,2,128,512]{4,3,2,1,0:T(8,128)(2,1)}), bf16[8,2,2,128,512]{4,3,2,1,0:T(8,128)(2,1)}, u32[]{:S(2)}, u32[]{:S(2)}) async-start(bf16[8,2,2,128,512]{4,3,2,1,0:T(8,128)(2,1)} %get-tuple-element.60), calls=%async_computation.7 | async-start | bytes 8388608 | tf_op jit(solution)/shard_map/all_to_all | solution.py:590
  259.3 138.7 %reduce-scatter.3.cloned.1.call-start = ((), (), s32[]{:S(2)}) async-start(), calls=%async_computation.17 | async-start | bytes 2621440 | tf_op jit(solution)/shard_map/reduce_scatter | solution.py:697
  308.4 54.1 %all-to-all-start.6 = ((bf16[8,2,2,128,512]{4,3,2,1,0:T(8,128)(2,1)}), bf16[8,2,2,128,512]{4,3,2,1,0:T(8,128)(2,1)}, u32[]{:S(2)}, u32[]{:S(2)}) async-start(bf16[8,2,2,128,512]{4,3,2,1,0:T(8,128)(2,1)} %get-tuple-element.54), calls=%async_computation.6 | async-start | bytes 8388608 | tf_op jit(solution)/shard_map/all_to_all | solution.py:590
  362.5 23.5 %all-to-all-start.12 = ((bf16[8,64,512]{2,1,0:T(8,128)(2,1)}), bf16[8,64,512]{2,1,0:T(8,128)(2,1)S(1)}, u32[]{:S(2)}, u32[]{:S(2)}) async-start(bf16[8,64,512]{2,1,0:T(8,128)(2,1)} %bitcast.71), calls=%async_computation.14 | async-start | bytes 1048576 | tf_op jit(solution)/shard_map/all_to_all | solution.py:590
  386.0 40.0 %all-to-all-start.8 = ((bf16[8,64,2176]{2,1,0:T(8,128)(2,1)}), bf16[8,64,2176]{2,1,0:T(8,128)(2,1)S(1)}, u32[]{:S(2)}, u32[]{:S(2)}) async-start(bf16[8,64,2176]{2,1,0:T(8,128)(2,1)} %bitcast.53), calls=%async_computation.8 | async-start | bytes 4456448 | tf_op jit(solution)/shard_map/all_to_all | solution.py:590
  426.0 13.2 %all-to-all-start.10 = ((bf16[8,16,2048]{2,1,0:T(8,128)(2,1)}), bf16[8,16,2048]{2,1,0:T(8,128)(2,1)S(1)}, u32[]{:S(2)}, u32[]{:S(2)}) async-start(bf16[8,16,2048]{2,1,0:T(8,128)(2,1)} %bitcast.72), calls=%async_computation.11 | async-start | bytes 1048576 | tf_op jit(solution)/shard_map/all_to_all | solution.py:590
  430.6 23.0 %copy-start.4 = (bf16[8,197,512]{2,1,0:T(8,128)(2,1)S(1)}, bf16[8,197,512]{2,1,0:T(8,128)(2,1)}, u32[]{:S(2)}) copy-start(bf16[8,197,512]{2,1,0:T(8,128)(2,1)} %get-tuple-element.161) | copy-start | bytes 4841476
  439.2 23.5 %all-to-all-start.9 = ((f32[4,16,2176]{2,1,0:T(8,128)}), f32[4,16,2176]{2,1,0:T(8,128)S(1)}, u32[]{:S(2)}, u32[]{:S(2)}) async-start(f32[4,16,2176]{2,1,0:T(8,128)} %bitcast.22), calls=%async_computation.9 | async-start | bytes 1114112 | tf_op jit(solution)/shard_map/all_to_all | solution.py:593
  449.9 5.4 %copy-start.7 = (f32[8,128]{1,0:T(8,128)}, f32[8,128]{1,0:T(8,128)S(1)}, u32[]{:S(2)}) copy-start(f32[8,128]{1,0:T(8,128)S(1)} %bitcast_reduce_fusion) | copy-start | bytes 12292
Sparse Core Ops, SparseCore 0:
  41.6 48.4 all-gather.2
  107.1 45.2 all-gather.4
  226.5 59.0 reduce-scatter.4
  287.9 43.1 reduce-scatter.2

commit v2 on v1

--- a/solution.py
+++ b/solution.py
@@ -13,6 +13,7 @@
 EXPERTS = 8
 MICRO = 4
 CAP = 128
+CHUNKS = (2, 2)
 PAIR = 2 * HEAD_DIM
 
 EPSILON = 1e-06
@@ -23,7 +24,8 @@
 
 ROW_GAIN1, ROW_BIAS1, ROW_QBIAS, ROW_VBIAS, ROW_OBIAS, ROW_GAIN2, ROW_BIAS2 = range(8, 15)
 SMALL = 128
-GRAD_ROWS = 16
+ROW_PROB, ROW_EOUT, ROW_EIN = 16, 32, 40
+BLOCK = 16
 COL_T0, COL_T1, COL_R0, COL_R1, COL_K0, COL_K1, COL_LIVE = range(7)
 VMEM_LIMIT = 60 * 1024 * 1024
 
@@ -227,7 +229,6 @@
 
 
 GROUP = 4
-FF_TILE = 512
 
 
 def expert_kernel(
@@ -237,8 +238,7 @@
     last,
     cnt_ref,
     x_ref,
-    w1_ref,
-    w2_ref,
+    w_ref,
     b1_ref,
     b2_ref,
     *rest,
@@ -246,15 +246,14 @@
     if has_acc:
         a1_ref, a2_ref, ab1_ref, ab2_ref = rest[:4]
         rest = rest[4:]
-    y_ref, g1_ref, g2_ref, gb1_ref, gb2_ref = rest[:5]
-    rest = rest[5:]
     if last:
-        s1, s2, order, xin, din, xout, dout = rest
+        y_ref, pack_ref, gb1_ref, gb2_ref, s1, s2, order, xin, din, xout, dout = rest
     else:
-        order, xin, din, xout, dout = rest
-        s1, s2 = g1_ref, g2_ref
+        y_ref, s1, s2, gb1_ref, gb2_ref, order, xin, din, xout, dout = rest
     width = x_ref.shape[-1]
-    ff = w1_ref.shape[1]
+    ff = b1_ref.shape[1]
+    half = w_ref.shape[1] // 2
+    per_tile = width // half
     if has_acc:
         s1[...] = a1_ref[...]
         s2[...] = a2_ref[...]
@@ -287,10 +286,10 @@
             din[j * CAP : (j + 1) * CAP, :] = x_ref[b // mbc, 1, b % mbc]
         rows_in, d_res = xin[...], din[...]
         gb2_ref[0:1, :] += jnp.sum(d_res.astype(F32), 0, keepdims=True)
-        for f in range(ff // FF_TILE):
-            cols = slice(f * FF_TILE, (f + 1) * FF_TILE)
-            w1 = w1_ref[:, cols]
-            w2 = w2_ref[cols, :]
+        for f in range(ff // width):
+            cols = slice(f * width, (f + 1) * width)
+            w1 = w_ref[:, f * BLOCK : (f + 1) * BLOCK, :].reshape(width, width)
+            w2 = w_ref[f * per_tile : (f + 1) * per_tile, half:, :].reshape(width, width)
             h = mm(rows_in, w1) + b1_ref[0:1, cols]
             bell = jnp.exp(-0.5 * h * h)
             t = 1.0 / (1.0 + (0.3275911 / math.sqrt(2.0)) * jnp.abs(h))
@@ -329,13 +328,19 @@
 
     lax.fori_loop(0, (live_total + GROUP - 1) // GROUP, one_group, 0)
     if last:
-        g1_ref[...] = s1[...].astype(BF)
-        g2_ref[...] = s2[...].astype(BF)
-
-
-def expert_call(m0, mbc, last, counts, x, w1, w2, b1, b2, acc):
-    width, ff = w1.shape
-    grad_type = BF if last else F32
+        blocks_of = width // BLOCK
+        for f in range(ff // width):
+            tile = s1[:, f * width : (f + 1) * width].astype(BF)
+            pack_ref[:, f * BLOCK : (f + 1) * BLOCK, :] = tile.reshape(blocks_of, BLOCK, width)
+        pack_ref[:, half:, :] = s2[...].astype(BF).reshape(blocks_of, half, width)
+
+
+def expert_call(m0, mbc, last, counts, x, weights, b1, b2, acc):
+    width, ff = weights.shape[2], b1.shape[1]
+    if last:
+        grads = [jax.ShapeDtypeStruct(weights.shape, BF)]
+    else:
+        grads = [jax.ShapeDtypeStruct((width, ff), F32), jax.ShapeDtypeStruct((ff, width), F32)]
     vm = pl.BlockSpec(memory_space=pltpu.VMEM)
     scratch = []
     if last:
@@ -349,12 +354,11 @@
     ]
     return pl.pallas_call(
         functools.partial(expert_kernel, m0, mbc, acc is not None, last),
-        in_specs=[pl.BlockSpec(memory_space=pltpu.SMEM)] + [vm] * (5 + (0 if acc is None else 4)),
-        out_specs=[vm] * 5,
+        in_specs=[pl.BlockSpec(memory_space=pltpu.SMEM)] + [vm] * (4 + (0 if acc is None else 4)),
+        out_specs=[vm] * (len(grads) + 3),
         out_shape=[
             jax.ShapeDtypeStruct(x.shape, BF),
-            jax.ShapeDtypeStruct((width, ff), grad_type),
-            jax.ShapeDtypeStruct((ff, width), grad_type),
+            *grads,
             jax.ShapeDtypeStruct((8, ff), F32),
             jax.ShapeDtypeStruct((8, width), F32),
         ],
@@ -364,7 +368,7 @@
             flops=mbc * 20 * 10**9, bytes_accessed=mbc * 10 * 10**6, transcendentals=0
         ),
         name="expert_both",
-    )(counts, x, w1, w2, b1, b2, *(() if acc is None else acc))
+    )(counts, x, weights, b1, b2, *(() if acc is None else acc))
 
 
 def backward_kernel(
@@ -372,6 +376,7 @@
     seq_len,
     pad_len,
     has_acc,
+    last,
     cnt_ref,
     img_ref,
     cot_ref,
@@ -385,12 +390,16 @@
     coef_ref,
     w_ref,
     small_ref,
+    extra_ref,
     *rest,
 ):
     if has_acc:
         accw_ref, accs_ref = rest[:2]
         rest = rest[4:]
-    out_ref, grad_ref, gw_ref, gs_ref, xs, cs, dq = rest
+    if last:
+        out_ref, grad_ref, pack_ref, xs, cs, dq, gw_ref, gs_ref = rest
+    else:
+        out_ref, grad_ref, gw_ref, gs_ref, xs, cs, dq = rest
     step = pl.program_id(0)
     width = xs.shape[1]
     alive = cnt_ref[0] > 2 * (m0 + step)
@@ -492,8 +501,38 @@
         for i in range(2):
             grad_ref[i] = d_tok[i * pad_len : i * pad_len + seq_len, :].astype(BF)
 
-
-def backward_call(m0, mbc, images, cotangent, count, meta, back, saved, coef, weights, small, acc):
+    if last:
+
+        @pl.when(step == pl.num_programs(0) - 1)
+        def _():
+            small_part = (gs_ref[...] + extra_ref[...]).T.astype(BF)
+            _, blocks, rows_of, wide = pack_ref.shape
+            for b in range(blocks):
+                for p in range(pack_ref.shape[0]):
+                    at = (b * pack_ref.shape[0] + p) * rows_of
+                    pack_ref[p, b, :, 0 : 4 * width] = gw_ref[at : at + rows_of, :].astype(BF)
+                    pack_ref[p, b, :, 4 * width :] = small_part[at : at + rows_of, :]
+
+
+def backward_call(
+    m0,
+    mbc,
+    last,
+    own_rows,
+    images,
+    cotangent,
+    count,
+    meta,
+    back,
+    saved,
+    coef,
+    weights,
+    small,
+    extra,
+    acc,
+):
+    lanes_of = EXPERTS if own_rows == BLOCK else 1
+    own_rows = own_rows if own_rows == BLOCK else BLOCK
     seq_len, width = images.shape[1], images.shape[2]
     rows = meta.shape[1]
     pad_len = rows // 2
@@ -515,8 +554,10 @@
         full_block(coef.shape),
         full_block(weights.shape),
         full_block(small.shape),
+        full_block(extra.shape),
     ]
-    args = [count, images, cotangent, meta, back, qkv, probs, att, mid, rp, coef, weights, small]
+    args = [count, images, cotangent, meta, back, qkv, probs, att, mid, rp]
+    args += [coef, weights, small, extra]
     aliases = {}
     if acc is not None:
         base = len(args)
@@ -524,27 +565,34 @@
         in_specs += [pl.BlockSpec(memory_space=pl.ANY)] * 2
         args += list(acc)
         aliases = {base + 2: 0, base + 3: 1}
+    sums = [(width, 4 * width), (SMALL, width)]
+    pack_shape = (lanes_of, width // (lanes_of * own_rows), own_rows, weights.shape[1])
+    if last:
+        grads = [jax.ShapeDtypeStruct(pack_shape, BF)]
+        held = [pltpu.VMEM(shape, F32) for shape in sums]
+    else:
+        grads = [jax.ShapeDtypeStruct(shape, F32) for shape in sums]
+        held = []
     return pl.pallas_call(
-        functools.partial(backward_kernel, m0, seq_len, pad_len, acc is not None),
+        functools.partial(backward_kernel, m0, seq_len, pad_len, acc is not None, last),
         grid=(mbc,),
         in_specs=in_specs,
         out_specs=[
             image_block,
             image_block,
-            full_block((width, 4 * width)),
-            full_block((GRAD_ROWS, width)),
-        ],
+        ]
+        + [full_block(g.shape) for g in grads],
         out_shape=[
             jax.ShapeDtypeStruct(images.shape, BF),
             jax.ShapeDtypeStruct(images.shape, BF),
-            jax.ShapeDtypeStruct((width, 4 * width), F32),
-            jax.ShapeDtypeStruct((GRAD_ROWS, width), F32),
-        ],
+        ]
+        + grads,
         scratch_shapes=[
             pltpu.VMEM((rows, width), F32),
             pltpu.VMEM((rows, width), F32),
             pltpu.VMEM((rows, 3 * width), BF),
-        ],
+        ]
+        + held,
         input_output_aliases=aliases,
         compiler_params=pltpu.CompilerParams(vmem_limit_bytes=VMEM_LIMIT),
         cost_estimate=pl.CostEstimate(
@@ -552,6 +600,77 @@
         ),
         name="dense_backward",
     )(*args)
+
+
+def finish_kernel(
+    got_ref,
+    bal_ref,
+    qkv_ref,
+    out_ref,
+    router_ref,
+    gain1_ref,
+    bias1_ref,
+    qv_ref,
+    obias_ref,
+    gain2_ref,
+    bias2_ref,
+    ein_ref,
+    eout_ref,
+    balance_ref,
+    turned,
+):
+    planes, rows, wide = got_ref.shape
+    width = out_ref.shape[1]
+    whole = got_ref[0]
+    for z in range(1, planes):
+        whole = whole + got_ref[z]
+    qkv_ref[...] = whole[:, : 3 * width]
+    out_ref[...] = whole[:, 3 * width : 4 * width]
+    turned[...] = jnp.zeros_like(turned)
+    turned[0:rows, :] = whole[:, 4 * width :]
+    balance_ref[...] = jnp.sum(turned[0:1, :] * bal_ref[0:1, :], -1, keepdims=True)
+    turned[...] = turned[...].T
+    router_ref[...] = turned[0:EXPERTS, 0:rows]
+    for row, ref in (
+        (ROW_GAIN1, gain1_ref),
+        (ROW_BIAS1, bias1_ref),
+        (ROW_OBIAS, obias_ref),
+        (ROW_GAIN2, gain2_ref),
+        (ROW_BIAS2, bias2_ref),
+    ):
+        ref[...] = turned[row : row + 1, 0:rows]
+    qv_ref[...] = turned[ROW_QBIAS : ROW_VBIAS + 1, 0:rows]
+    eout_ref[...] = turned[ROW_EOUT : ROW_EOUT + EXPERTS, 0:rows]
+    for c in range(ein_ref.shape[1] // rows):
+        at = ROW_EIN + c * EXPERTS
+        ein_ref[:, c * rows : (c + 1) * rows] = turned[at : at + EXPERTS, 0:rows]
+
+
+def finish_call(got, bal, width, ff_rows):
+    rows = got.shape[1]
+    shapes = [
+        (rows, 3 * width),
+        (rows, width),
+        (EXPERTS, rows),
+        (1, rows),
+        (1, rows),
+        (2, rows),
+        (1, rows),
+        (1, rows),
+        (1, rows),
+        (EXPERTS, ff_rows),
+        (EXPERTS, rows),
+        (1, 1),
+    ]
+    vm = pl.BlockSpec(memory_space=pltpu.VMEM)
+    return pl.pallas_call(
+        finish_kernel,
+        in_specs=[vm] * 2,
+        out_specs=[vm] * len(shapes),
+        out_shape=[jax.ShapeDtypeStruct(shape, F32) for shape in shapes],
+        scratch_shapes=[pltpu.VMEM((SMALL, SMALL), F32)],
+        name="finish",
+    )(got, bal)
 
 
 def shards(
@@ -595,6 +714,24 @@
     def z_gather(v):
         return lax.all_gather(v, "dp", axis=0, tiled=True, axis_index_groups=z_groups)
 
+    parts = ff // width
+    expert_pack = jnp.concatenate(
+        [
+            expert_in.reshape(EXPERTS, rows, parts, width)
+            .transpose(0, 2, 1, 3)
+            .reshape(EXPERTS, ff_rows, width),
+            expert_out,
+        ],
+        1,
+    )
+    expert_pack = plane_swap(expert_pack)
+
+    live_img = (jnp.arange(slots) < image_count[0]).astype(F32)
+    live_tok = jnp.broadcast_to(live_img[:, None, None], (slots, seq_len, 1))
+    hits = (expert_index[..., None] == jnp.arange(EXPERTS)).astype(F32) * live_tok[..., None]
+    local_counts = jnp.sum(hits, axis=(0, 1, 2))
+    high = jnp.floor(local_counts * (1.0 / 128.0))
+    told = jnp.concatenate([high, local_counts - 128.0 * high, image_count.astype(F32)]).astype(BF)
     small_cols = jnp.concatenate(
         [
             router_weight,
@@ -604,10 +741,18 @@
             out_bias[:, None],
             ln2_gain[:, None],
             ln2_bias[:, None],
-            jnp.zeros((rows, SMALL - 15), BF),
+            jnp.zeros((rows, 1), BF),
+            expert_in_bias.reshape(EXPERTS, parts, rows).transpose(2, 0, 1).reshape(rows, -1),
+            expert_out_bias.T,
+            jnp.broadcast_to(told[None], (rows, 2 * EXPERTS + 1)),
         ],
         1,
     )
+    col_in_bias = 2 * EXPERTS
+    col_out_bias = col_in_bias + EXPERTS * parts
+    col_counts = col_out_bias + EXPERTS
+    col_images = col_counts + 2 * EXPERTS
+    small_cols = jnp.pad(small_cols, ((0, 0), (0, SMALL - small_cols.shape[1])))
     packed = jnp.concatenate([qkv_weight, out_weight, small_cols], 1)
     wide = packed.shape[1]
     packed = z_gather(packed)
@@ -617,11 +762,7 @@
     )
     small = weights[:, 4 * width :].astype(F32).T
 
-    live_img = jnp.arange(slots) < image_count[0]
-    live_tok = jnp.broadcast_to(live_img[:, None, None], (slots, seq_len, 1)).astype(F32)
     target = jnp.where(keep == 1, expert_index * CAP + expert_slot, -1).astype(F32)
-    hits = (expert_index[..., None] == jnp.arange(EXPERTS)).astype(F32) * live_tok[..., None]
-    local_counts = jnp.sum(hits, axis=(0, 1, 2))
     meta = jnp.concatenate(
         [
             target,
@@ -638,135 +779,171 @@
     ).reshape(MICRO, mb * pad_len, 8)
     lane_t = meta.transpose(0, 2, 1)
 
-    high = jnp.floor(local_counts * (1.0 / 128.0))
-    told = jnp.concatenate(
-        [
-            expert_in_bias,
-            expert_out_bias,
-            jnp.broadcast_to(
-                jnp.concatenate(
-                    [high, local_counts - 128.0 * high, image_count.astype(F32)]
-                ).astype(BF)[None],
-                (EXPERTS, 2 * EXPERTS + 1),
-            ),
-        ],
-        1,
-    )
-    told = jnp.pad(told, ((0, 0), (0, 128 - told.shape[1])))
-    told = jnp.broadcast_to(told[None], (planes,) + told.shape).reshape(total, 128)
-    heard = lax.all_to_all(told, "dp", 0, 0, tiled=True).astype(F32)
-    in_bias = heard[:, :ff_rows].reshape(1, ff)
-    out_bias_e = heard[:, ff_rows : ff_rows + rows].reshape(1, width)
-    base = ff_rows + rows
-    tail = heard[:, base : base + 2 * EXPERTS + 1]
-    counts_all = jnp.sum(tail[:, :EXPERTS] * 128.0 + tail[:, EXPERTS : 2 * EXPERTS], 0)
-    all_images = tail[:, 2 * EXPERTS]
-    live_total = jnp.sum(all_images) * float(seq_len)
-    plane_id = lax.axis_index("dp") // EXPERTS
-    plane_counts = lax.dynamic_slice(all_images, (plane_id * EXPERTS,), (EXPERTS,)).astype(
-        jnp.int32
-    )
+    me = lax.axis_index("dp")
+    in_bias = lax.dynamic_slice_in_dim(small, col_in_bias + parts * (me % EXPERTS), parts, 0)
+    in_bias = in_bias.reshape(parts, total, rows).transpose(1, 0, 2).reshape(1, ff)
+    out_bias_e = lax.dynamic_slice_in_dim(small, col_out_bias + me % EXPERTS, 1, 0)
+    sums = jnp.sum(small[col_counts : col_images + 1], 1) * (1.0 / rows)
+    counts_all = sums[:EXPERTS] * 128.0 + sums[EXPERTS : 2 * EXPERTS]
+    live_total = sums[2 * EXPERTS] * float(seq_len)
+    plane_counts = lax.dynamic_slice_in_dim(
+        small[col_images], (me // EXPERTS) * (EXPERTS * rows), EXPERTS * rows, 0
+    )
+    plane_counts = plane_counts.reshape(EXPERTS, rows)[:, 0].astype(jnp.int32)
     coef = jnp.pad(BALANCE_WEIGHT * EXPERTS * counts_all / live_total, (0, SMALL - EXPERTS))
     coef = jnp.broadcast_to(coef[None], (8, SMALL))
     in_bias = jnp.broadcast_to(in_bias, (8, ff))
     out_bias_e = jnp.broadcast_to(out_bias_e, (8, width))
 
-    w1 = z_gather(plane_swap(expert_in).reshape(EXPERTS * rows, ff))
-    w2 = z_gather(plane_swap(expert_out).reshape(EXPERTS * ff_rows, width))
-
-    chunks = 2
-    mbc = MICRO // chunks
+    expert_pack = z_gather(expert_pack)
+    if rows != BLOCK:
+        blocks = width // BLOCK
+        expert_pack = jnp.concatenate(
+            [
+                expert_pack[:, :ff_rows]
+                .reshape(blocks, total // blocks, parts, rows, width)
+                .transpose(0, 2, 1, 3, 4)
+                .reshape(blocks, parts * BLOCK, width),
+                expert_pack[:, ff_rows:].reshape(blocks, parts * BLOCK, width),
+            ],
+            1,
+        )
+
+    spans = []
+    for size in CHUNKS:
+        spans.append((sum(span[1] for span in spans), size))
     saved, sent, prob_sums = [], [], []
-    for c in range(chunks):
+    for m0, mbc in spans:
         xd, qkv, probs, att, mid, rp, prob = forward_call(
-            c * mbc, mbc, images, cotangent, image_count, lane_t, meta, weights, small
+            m0, mbc, images, cotangent, image_count, lane_t, meta, weights, small
         )
         saved.append((qkv, probs, att, mid, rp))
         prob_sums.append(prob[0, :EXPERTS])
         sent.append(plane_swap(xd))
     acc = None
     back = []
-    for c in range(chunks):
+    for (m0, mbc), rows_in in zip(spans, sent):
         y, *acc = expert_call(
-            c * mbc, mbc, c == chunks - 1, plane_counts, sent[c], w1, w2, in_bias, out_bias_e, acc
+            m0,
+            mbc,
+            m0 + mbc == MICRO,
+            plane_counts,
+            rows_in,
+            expert_pack,
+            in_bias,
+            out_bias_e,
+            acc,
         )
         back.append(plane_swap(y))
-    g1, g2, gb1, gb2 = acc
-
-    def z_reduce(v):
-        return lax.psum_scatter(
-            v, "dp", scatter_dimension=0, tiled=True, axis_index_groups=z_groups
+    expert_grads, gb1, gb2 = acc
+
+    if rows != BLOCK:
+        expert_grads = jnp.concatenate(
+            [
+                expert_grads[:, : parts * BLOCK]
+                .reshape(blocks, parts, total // blocks, rows, width)
+                .transpose(0, 2, 1, 3, 4)
+                .reshape(total, ff_rows, width),
+                expert_grads[:, parts * BLOCK :].reshape(total, ff_rows, width),
+            ],
+            1,
         )
-
-    expert_in_grad = plane_swap(z_reduce(g1).reshape(EXPERTS, rows, ff)).astype(F32)
-    expert_out_grad = plane_swap(z_reduce(g2).reshape(EXPERTS, ff_rows, width)).astype(F32)
-    bias_told = jnp.concatenate([gb1[0].reshape(total, ff_rows), gb2[0].reshape(total, rows)], 1)
-    bias_told = jnp.pad(bias_told, ((0, 0), (0, 128 - bias_told.shape[1])))
-    bias_heard = lax.all_to_all(bias_told, "dp", 0, 0, tiled=True)
-    bias_heard = jnp.sum(bias_heard.reshape(planes, EXPERTS, 128), 0)
-    expert_in_bias_grad = bias_heard[:, :ff_rows]
-    expert_out_bias_grad = bias_heard[:, ff_rows : ff_rows + rows]
+    expert_grads = lax.psum_scatter(
+        expert_grads, "dp", scatter_dimension=0, tiled=True, axis_index_groups=z_groups
+    )
+    expert_grads = plane_swap(expert_grads).astype(F32)
+    expert_in_grad = (
+        expert_grads[:, :ff_rows]
+        .reshape(EXPERTS, parts, rows, width)
+        .transpose(0, 2, 1, 3)
+        .reshape(EXPERTS, rows, ff)
+    )
+    expert_out_grad = expert_grads[:, ff_rows:]
+
+    prob_sum = prob_sums[0]
+    for piece in prob_sums[1:]:
+        prob_sum = prob_sum + piece
+    p_hi = prob_sum.astype(BF).astype(F32)
+    mine = (jnp.arange(EXPERTS) == me % EXPERTS).astype(F32)
+    e_in = gb1[0].reshape(total, parts, rows).transpose(1, 0, 2).reshape(parts, 1, width)
+    extra = jnp.concatenate(
+        [
+            jnp.zeros((ROW_PROB, width), F32),
+            jnp.broadcast_to(
+                jnp.concatenate([p_hi, prob_sum - p_hi])[:, None], (2 * EXPERTS, width)
+            ),
+            mine[:, None] * gb2[0:1],
+            (mine[None, :, None] * e_in).reshape(parts * EXPERTS, width),
+            jnp.zeros((SMALL - ROW_EIN - parts * EXPERTS, width), F32),
+        ],
+        0,
+    )
 
     acc = None
-    for c in range(chunks):
-        block_out, image_grad, gw, gs = backward_call(
-            c * mbc,
+    for (m0, mbc), returned, kept in zip(spans, back, saved):
+        block_out, image_grad, *acc = backward_call(
+            m0,
             mbc,
+            m0 + mbc == MICRO,
+            rows,
             images,
             cotangent,
             image_count,
             meta,
-            back[c],
-            saved[c],
+            returned,
+            kept,
             coef,
             weights,
             small,
-            acc,
+            extra,
+            None if acc is None else (*acc, block_out, image_grad),
         )
-        acc = (gw, gs, block_out, image_grad)
-
-    prob_sum = prob_sums[0]
-    for piece in prob_sums[1:]:
-        prob_sum = prob_sum + piece
-    p_hi = prob_sum.astype(BF)
-    p_mid = (prob_sum - p_hi.astype(F32)).astype(BF)
-    extra = jnp.broadcast_to(jnp.concatenate([p_hi, p_mid])[None], (width, 2 * EXPERTS))
-    grads = jnp.concatenate(
-        [
-            gw.astype(BF),
-            gs.T.astype(BF),
-            extra,
-            jnp.zeros((width, SMALL - GRAD_ROWS - 2 * EXPERTS), BF),
-        ],
-        1,
-    )
-    grads = grads.reshape(planes, EXPERTS, rows, wide).transpose(1, 0, 2, 3)
+
+    grads = acc[0]
+    if rows != BLOCK:
+        grads = grads.reshape(planes, EXPERTS, rows, wide).transpose(1, 0, 2, 3)
     grads = plane_swap(grads.reshape(EXPERTS, planes * rows, wide))
-    grads = jnp.sum(grads.astype(F32), 0).reshape(planes, rows, wide)
-    grads = jnp.sum(z_swap(grads), 0)
-    small_grads = grads[:, 4 * width :]
-    prob_all = (
-        small_grads[0, GRAD_ROWS : GRAD_ROWS + EXPERTS]
-        + small_grads[0, GRAD_ROWS + EXPERTS : GRAD_ROWS + 2 * EXPERTS]
-    )
-    balance = EXPERTS * jnp.sum(counts_all / live_total * prob_all / live_total)
+    grads = lax.psum_scatter(
+        jnp.sum(grads.astype(F32), 0),
+        "dp",
+        scatter_dimension=0,
+        tiled=True,
+        axis_index_groups=z_groups,
+    )
+    bal = EXPERTS * counts_all / live_total / live_total
+    bal = jnp.concatenate([jnp.zeros((ROW_PROB,), F32), bal, bal])
+    bal = jnp.broadcast_to(jnp.pad(bal, (0, SMALL - bal.shape[0]))[None], (8, SMALL))
+    (
+        qkv_grad,
+        out_grad,
+        router_grad,
+        gain1_grad,
+        bias1_grad,
+        qv_grad,
+        obias_grad,
+        gain2_grad,
+        bias2_grad,
+        ein_grad,
+        eout_grad,
+        balance,
+    ) = finish_call(grads[None], bal, width, ff_rows)
     return (
         block_out,
         image_grad,
-        balance,
-        small_grads[:, ROW_GAIN1],
-        small_grads[:, ROW_BIAS1],
-        grads[:, : 3 * width],
-        small_grads[:, ROW_QBIAS : ROW_VBIAS + 1].T,
-        grads[:, 3 * width : 4 * width],
-        small_grads[:, ROW_OBIAS],
-        small_grads[:, ROW_GAIN2],
-        small_grads[:, ROW_BIAS2],
-        small_grads[:, :EXPERTS],
+        balance.reshape(()),
+        gain1_grad.reshape(rows),
+        bias1_grad.reshape(rows),
+        qkv_grad,
+        qv_grad,
+        out_grad,
+        obias_grad.reshape(rows),
+        gain2_grad.reshape(rows),
+        bias2_grad.reshape(rows),
+        router_grad.T,
         expert_in_grad,
-        expert_in_bias_grad,
+        ein_grad,
         expert_out_grad,
-        expert_out_bias_grad,
+        eout_grad,
     )
 
 

time: 484 us -> 402 us (0.83)
  starting transfers between devices: 66.3 us -> 32 us
  waiting for transfers between devices: 179 us -> 146 us
  local copies, waits for them, and re-layouts: 35.2 us -> 23.3 us
  blocking collectives: 40.8 us -> 51.8 us
  Pallas kernels: 123 us -> 116 us
  other arithmetic: 12.8 us -> 7.58 us
    all_to_all x10 -> x7, waiting for transfers between devices: 169 us -> 120 us  [plane_swap(): lax.all_to_all(v, 'dp', 0, 0, tiled=True, axis_index_groups=plane_groups)]
    reduce_scatter x2, waiting for transfers between devices: 0.01 us -> 26 us  [the longest x1 26 us: shards(): lax.psum_scatter(jnp.sum(grads.astype(F32), 0), 'dp', scatter_dimension=0...]
    all_to_all x10 -> x7, starting transfers between devices: 50.6 us -> 31.5 us  [plane_swap(): lax.all_to_all(v, 'dp', 0, 0, tiled=True, axis_index_groups=plane_groups)]
    all_to_all x2 -> x0, starting transfers between devices: 15.1 us -> none  [the longest x1 10.7 us: z_swap(): return lax.all_to_all(v, 'dp', 0, 0, tiled=True, axis_index_groups=z_groups)]
    all_to_all x1, blocking collectives: 26.5 us -> 37.5 us  [plane_swap(): lax.all_to_all(v, 'dp', 0, 0, tiled=True, axis_index_groups=plane_groups)]
    all_to_all x2 -> x0, waiting for transfers between devices: 10.1 us -> none  [the longest x1 5.23 us: z_swap(): return lax.all_to_all(v, 'dp', 0, 0, tiled=True, axis_index_groups=z_groups)]
    pallas_call x2, Pallas kernels: 63.1 us -> 54.4 us  [expert_call(): pl.pallas_call(functools.partial(expert_kernel, m0, mbc, acc is not None,...]
    convert_element_type x9 -> x5, other arithmetic: 8.84 us -> 1.38 us  [the longest x1 0.71 us: shards(): p_hi = prob_sum.astype(BF).astype(F32)]
  transfers between devices with their start and end apart: 16 -> 10, of which waited for: 9 -> 6; matrix products, arithmetic and copies ran while one was open for 8% -> 6% of each run, Pallas kernels for 22% -> 30%
where the time goes in v2:
time: 402 us; the launch traced here: 394 us
  waiting for transfers between devices  146 us (36%)
  Pallas kernels  116 us (29%)
  blocking collectives  51.8 us (13%)
  starting transfers between devices  32 us (8%)
  local copies, waits for them, and re-layouts  23.3 us (6%)
  between operations  17 us (4%)
  other arithmetic  7.58 us (2%)
    all_to_all x7, waiting for transfers between devices, plane_swap(): lax.all_to_all(v, 'dp', 0, 0, tiled=True, axis_index_groups=plane_groups)  120 us
    pallas_call x2, Pallas kernels, expert_call(): pl.pallas_call(functools.partial(expert_kernel, m0, mbc, acc is not None,...  54.4 us
    all_to_all x1, blocking collectives, plane_swap(): lax.all_to_all(v, 'dp', 0, 0, tiled=True, axis_index_groups=plane_groups)  37.5 us
    pallas_call x2, Pallas kernels, backward_call(): pl.pallas_call(functools.partial(backward_kernel, m0, seq_len, pad_len, a...  35.9 us
    all_to_all x7, starting transfers between devices, plane_swap(): lax.all_to_all(v, 'dp', 0, 0, tiled=True, axis_index_groups=plane_groups)  31.5 us
    reduce_scatter x1, waiting for transfers between devices, shards(): lax.psum_scatter(jnp.sum(grads.astype(F32), 0), 'dp', scatter_dimension=0...  26 us
    pallas_call x2, Pallas kernels, forward_call(): pl.pallas_call(functools.partial(forward_kernel, m0, seq_len, pad_len), g...  24.5 us
    all_gather x1, blocking collectives, z_gather(): lax.all_gather(v, 'dp', axis=0, tiled=True, axis_index_groups=z_groups)  14.4 us
  transfers between devices with their start and end apart: 10, of which 6 were waited for; matrix products, arithmetic and copies ran while one was open for 6% of the time, Pallas kernels for 30%

profile of v2, /device:TPU:0, one launch (start us, length us, event | category | flops | bytes accessed | tf_op | source)
XLA Modules:
  0.0 394.1 jit_solution(10247032526008788114)
XLA Ops:
  7.2 1.1 copy.149
  8.4 2.1 pad_maximum_fusion
  10.6 5.2 %all-to-all-start.2 = ((bf16[8,128,512]{2,1,0:T(8,128)(2,1)}), bf16[8,128,512]{2,1,0:T(8,128)(2,1)S(1)}, u32[]{:S(2)}, u32[]{:S(2)}) async-start(bf16[8,128,512]{2,1,0:T(8,128)(2,1)} %pad_maximum_fusion), calls=%async_computation.2 | async-start | bytes 2097152 | tf_op jit(solution)/shard_map/all_to_all | solution.py:709
  17.8 14.4 %all_gather.6 = bf16[64,2176]{1,0:T(8,128)(2,1)S(1)} all-gather(bf16[16,2176]{1,0:T(8,128)(2,1)S(1)} %fusion.1), channel_id=1, replica_groups={{0,8,16,24},{1,9,17,25},{2,10,18,26},{3,11,19,27},{4,12,20,28},{5,13,21..., dimensions={0}, use_global_device_ids=true | all-gather | bytes 348160 | tf_op jit(solution)/shard_map/all_gather | solution.py:715
  32.2 1.7 broadcast_in_dim.98
  33.9 4.0 %all-to-all-start = ((bf16[8,64,2176]{2,1,0:T(8,128)(2,1)}), bf16[8,64,2176]{2,1,0:T(8,128)(2,1)S(1)}, u32[]{:S(2)}, u32[]{:S(2)}) async-start(bf16[8,64,2176]{2,1,0:T(8,128)(2,1)} %broadcast_in_dim.98), calls=%async_computation | async-start | bytes 4456448 | tf_op jit(solution)/shard_map/all_to_all | solution.py:709
  38.0 3.2 copy.140.img_ref
  41.3 1.7 copy.141.cot_ref
  44.7 21.3 %all-to-all-done = bf16[8,64,2176]{2,1,0:T(8,128)(2,1)S(1)} async-done(((bf16[8,64,2176]{2,1,0:T(8,128)(2,1)}), bf16[8,64,2176]{2,1,0:T(8,128)(2,1)S(1)}, u32[]{:S(2)}, u32[]{:S(2)}) %all-to-all-start) | async-done | bytes 2228256 | tf_op jit(solution)/shard_map/all_to_all | solution.py:709
  66.2 1.4 copy-done.2
  68.4 17.5 %dense_forward.3 = (bf16[8,2,2,128,512]{4,3,2,1,0:T(8,128)(2,1)}, bf16[2,416,1536]{2,1,0:T(8,128)(2,1)}, bf16[2,2,4,416,208]{4,3,2,1,0:T(8,128)(2,1)}, bf16[2,41...) custom-call(s32[1]{0:T(128)} %copy.156.cnt_ref, ...), custom_call_target="tpu_custom_call" | custom-call | flops 24000000000 | bytes 20000000 | tf_op jit(solution)/shard_map/dense_forward/pallas_call | solution.py:192
  85.9 5.0 %all-to-all-start.3 = ((bf16[8,2,2,128,512]{4,3,2,1,0:T(8,128)(2,1)}), bf16[8,2,2,128,512]{4,3,2,1,0:T(8,128)(2,1)}, u32[]{:S(2)}, u32[]{:S(2)}) async-start(bf16[8,2,2,128,512]{4,3,2,1,0:T(8,128)(2,1)} %get-tuple-element.59), calls=%async_computation.3 | async-start | bytes 8388608 | tf_op jit(solution)/shard_map/all_to_all | solution.py:709
  95.0 7.0 %dense_forward.2 = (bf16[8,2,2,128,512]{4,3,2,1,0:T(8,128)(2,1)}, bf16[2,416,1536]{2,1,0:T(8,128)(2,1)}, bf16[2,2,4,416,208]{4,3,2,1,0:T(8,128)(2,1)}, bf16[2,41...) custom-call(s32[1]{0:T(128)} %copy.156.cnt_ref, ...), custom_call_target="tpu_custom_call" | custom-call | flops 24000000000 | bytes 20000000 | tf_op jit(solution)/shard_map/dense_forward/pallas_call | solution.py:192
  104.2 35.9 %all-to-all-done.3.x_ref = bf16[8,2,2,128,512]{4,3,2,1,0:T(8,128)(2,1)} async-done(((bf16[8,2,2,128,512]{4,3,2,1,0:T(8,128)(2,1)}), bf16[8,2,2,128,512]{4,3,2,1,0:T(8,128)(2,1)}, u32[]{:S(2)}, u32[]{:S(2)}) %all-to-all-start.3) | async-done | bytes 4194336 | tf_op jit(solution)/shard_map/all_to_all | solution.py:709
  140.1 4.6 %all-to-all-start.1 = ((bf16[8,2,2,128,512]{4,3,2,1,0:T(8,128)(2,1)}), bf16[8,2,2,128,512]{4,3,2,1,0:T(8,128)(2,1)}, u32[]{:S(2)}, u32[]{:S(2)}) async-start(bf16[8,2,2,128,512]{4,3,2,1,0:T(8,128)(2,1)} %get-tuple-element.58), calls=%async_computation.1 | async-start | bytes 8388608 | tf_op jit(solution)/shard_map/all_to_all | solution.py:709
  146.0 35.4 %expert_both.2 = (bf16[8,2,2,128,512]{4,3,2,1,0:T(8,128)(2,1)}, f32[512,2048]{1,0:T(8,128)}, f32[2048,512]{1,0:T(8,128)}, f32[8,2048]{1,0:T(8,128)}, f32[8,512]{1,0:T(8,128)}) custom-call(s32[8]{0:T(128)} %convert_reduce_fusion.1.cnt_ref, bf16[8,2,2,128,512]{4,3,2,1,0:T(8,128)(2,1)} %all-to-all-done.3.x_ref, ...), custom_call_target="tpu_custom_call" | custom-call | flops 40000000000 | bytes 20000000 | tf_op jit(solution)/shard_map/expert_both/pallas_call | solution.py:355
  181.4 12.4 %all-to-all-done.1.x_ref = bf16[8,2,2,128,512]{4,3,2,1,0:T(8,128)(2,1)} async-done(((bf16[8,2,2,128,512]{4,3,2,1,0:T(8,128)(2,1)}), bf16[8,2,2,128,512]{4,3,2,1,0:T(8,128)(2,1)}, u32[]{:S(2)}, u32[]{:S(2)}) %all-to-all-start.1) | async-done | bytes 4194336 | tf_op jit(solution)/shard_map/all_to_all | solution.py:709
  193.8 4.6 %all-to-all-start.5 = ((bf16[8,2,2,128,512]{4,3,2,1,0:T(8,128)(2,1)}), bf16[8,2,2,128,512]{4,3,2,1,0:T(8,128)(2,1)}, u32[]{:S(2)}, u32[]{:S(2)}) async-start(bf16[8,2,2,128,512]{4,3,2,1,0:T(8,128)(2,1)} %get-tuple-element.74), calls=%async_computation.5 | async-start | bytes 8388608 | tf_op jit(solution)/shard_map/all_to_all | solution.py:709
  198.5 18.9 %expert_both.3 = (bf16[8,2,2,128,512]{4,3,2,1,0:T(8,128)(2,1)}, bf16[32,128,512]{2,1,0:T(8,128)(2,1)}, f32[8,2048]{1,0:T(8,128)}, f32[8,512]{1,0:T(8,128)}) custom-call(s32[8]{0:T(128)} %convert_reduce_fusion.1.cnt_ref, bf16[8,2,2,128,512]{4,3,2,1,0:T(8,128)(2,1)} %all-to-all-done.1.x_ref, bf16[32,128,512]{2,1,0:T(8,128)(2,1)} %all-gather.2.cloned.1.call-done.w_ref, ...), custom_call_target="tpu_custom_call" | custom-call | flops 40000000000 | bytes 20000000 | tf_op jit(solution)/shard_map/expert_both/pallas_call | solution.py:355
  219.4 28.1 %all-to-all-done.5.y_ref = bf16[8,2,2,128,512]{4,3,2,1,0:T(8,128)(2,1)} async-done(((bf16[8,2,2,128,512]{4,3,2,1,0:T(8,128)(2,1)}), bf16[8,2,2,128,512]{4,3,2,1,0:T(8,128)(2,1)}, u32[]{:S(2)}, u32[]{:S(2)}) %all-to-all-start.5) | async-done | bytes 4194336 | tf_op jit(solution)/shard_map/all_to_all | solution.py:709
  247.5 4.6 %all-to-all-start.4 = ((bf16[8,2,2,128,512]{4,3,2,1,0:T(8,128)(2,1)}), bf16[8,2,2,128,512]{4,3,2,1,0:T(8,128)(2,1)}, u32[]{:S(2)}, u32[]{:S(2)}) async-start(bf16[8,2,2,128,512]{4,3,2,1,0:T(8,128)(2,1)} %get-tuple-element.64), calls=%async_computation.4 | async-start | bytes 8388608 | tf_op jit(solution)/shard_map/all_to_all | solution.py:709
  253.2 26.1 %dense_backward.2 = (bf16[8,197,512]{2,1,0:T(8,128)(2,1)}, bf16[8,197,512]{2,1,0:T(8,128)(2,1)}, f32[512,2048]{1,0:T(8,128)}, f32[128,512]{1,0:T(8,128)}) custom-call(s32[1]{0:T(128)} %copy.156.cnt_ref, bf16[8,197,512]{2,1,0:T(8,128)(2,1)} %copy.140.img_ref, bf16[8,197,512]{2,1,0:T(8,128)(2,1)} %copy.141.cot_ref, f32[4,416,8]{2,1,0:T(8,128)} %bitcast.66, ...), custom_call_target="tpu_custom_call" | custom-call | flops 40000000000 | bytes 20000000 | tf_op jit(solution)/shard_map/dense_backward/pallas_call | solution.py:576
  279.2 22.0 %all-to-all-done.4.y_ref = bf16[8,2,2,128,512]{4,3,2,1,0:T(8,128)(2,1)} async-done(((bf16[8,2,2,128,512]{4,3,2,1,0:T(8,128)(2,1)}), bf16[8,2,2,128,512]{4,3,2,1,0:T(8,128)(2,1)}, u32[]{:S(2)}, u32[]{:S(2)}) %all-to-all-start.4) | async-done | bytes 4194336 | tf_op jit(solution)/shard_map/all_to_all | solution.py:709
  301.2 9.8 %dense_backward.3 = (bf16[8,197,512]{2,1,0:T(8,128)(2,1)}, bf16[8,197,512]{2,1,0:T(8,128)(2,1)}, bf16[8,4,16,2176]{3,2,1,0:T(8,128)(2,1)}) custom-call(s32[1]{0:T(128)} %copy.156.cnt_ref, bf16[8,197,512]{2,1,0:T(8,128)(2,1)} %copy.140.img_ref, bf16[8,197,512]{2,1,0:T(8,128)(2,1)} %copy.141.cot_ref, ...), custom_call_target="tpu_custom_call", output_to_operand_aliasing={{0}: (16, {}), {1}: (17, {})} | custom-call | flops 40000000000 | bytes 20000000 | tf_op jit(solution)/shard_map/dense_backward/pallas_call | solution.py:576
  311.1 37.5 %all_to_all.40 = bf16[8,64,2176]{2,1,0:T(8,128)(2,1)S(1)} all-to-all(bf16[8,64,2176]{2,1,0:T(8,128)(2,1)} %bitcast.73), channel_id=1, replica_groups={{0,1,2,3,4,5,6,7},{8,9,10,11,12,13,14,15},{16,17,18,19,20,21,22,23},{24..., dimensions={0} | all-to-all | bytes 4456448 | tf_op jit(solution)/shard_map/all_to_all | solution.py:709
  348.5 1.1 convert_reduce_fusion
  349.7 3.6 all-to-all-start.7
  353.4 1.7 copy.143
  355.1 1.7 copy.144
  356.7 26.0 %reduce-scatter.3.cloned.1.call-done = f32[16,2176]{1,0:T(8,128)} async-done(((f32[64,2176]{1,0:T(8,128)}), f32[16,2176]{1,0:T(8,128)}) %reduce-scatter.3.cloned.1.call-update) | async-done | bytes 139280 | tf_op jit(solution)/shard_map/reduce_scatter | solution.py:906
  383.3 1.7 finish.1
  385.0 1.3 fusion.7
  (124 shorter events, 14.5 us)
Async XLA Ops:
  8.3 8.1 %copy-start.13 = (bf16[16,8]{0,1:T(8,128)(2,1)S(1)}, bf16[16,8]{0,1:T(8,128)(2,1)}, u32[]{:S(2)}) copy-start(bf16[16,8]{0,1:T(8,128)(2,1)} %param.34) | copy-start | bytes 772
  8.3 8.2 %copy-start.17 = (bf16[16]{0:T(256)(128)(2,1)S(1)}, bf16[16]{0:T(256)(128)(2,1)}, u32[]{:S(2)}) copy-start(bf16[16]{0:T(256)(128)(2,1)} %param.26) | copy-start | bytes 100
  8.3 8.3 %copy-start.18 = (bf16[16]{0:T(256)(128)(2,1)S(1)}, bf16[16]{0:T(256)(128)(2,1)}, u32[]{:S(2)}) copy-start(bf16[16]{0:T(256)(128)(2,1)} %param.27) | copy-start | bytes 100
  8.3 8.4 %copy-start.19 = (bf16[2,16]{1,0:T(2,128)(2,1)S(1)}, bf16[2,16]{1,0:T(2,128)(2,1)}, u32[]{:S(2)}) copy-start(bf16[2,16]{1,0:T(2,128)(2,1)} %param.29) | copy-start | bytes 196
  8.3 8.5 %copy-start.20 = (bf16[16]{0:T(256)(128)(2,1)S(1)}, bf16[16]{0:T(256)(128)(2,1)}, u32[]{:S(2)}) copy-start(bf16[16]{0:T(256)(128)(2,1)} %param.31) | copy-start | bytes 100
  8.3 8.5 %copy-start.21 = (bf16[16]{0:T(256)(128)(2,1)S(1)}, bf16[16]{0:T(256)(128)(2,1)}, u32[]{:S(2)}) copy-start(bf16[16]{0:T(256)(128)(2,1)} %param.32) | copy-start | bytes 100
  8.4 8.6 %copy-start.22 = (bf16[16]{0:T(256)(128)(2,1)S(1)}, bf16[16]{0:T(256)(128)(2,1)}, u32[]{:S(2)}) copy-start(bf16[16]{0:T(256)(128)(2,1)} %param.33) | copy-start | bytes 100
  8.4 8.7 %copy-start.14 = (bf16[8,64]{1,0:T(8,128)(2,1)S(1)}, bf16[8,64]{1,0:T(8,128)(2,1)}, u32[]{:S(2)}) copy-start(bf16[8,64]{1,0:T(8,128)(2,1)} %param.36) | copy-start | bytes 3076
  8.4 8.9 %copy-start.15 = (bf16[8,16]{1,0:T(8,128)(2,1)S(1)}, bf16[8,16]{1,0:T(8,128)(2,1)}, u32[]{:S(2)}) copy-start(bf16[8,16]{1,0:T(8,128)(2,1)} %param.38) | copy-start | bytes 772
  8.4 8.9 %copy-start.7 = (s32[8,197,2]{1,2,0:T(2,128)S(1)}, s32[8,197,2]{1,2,0:T(2,128)}, u32[]{:S(2)}) copy-start(s32[8,197,2]{1,2,0:T(2,128)} %param.22) | copy-start | bytes 37828
  8.4 9.4 %copy-start.8 = (bf16[16,1536]{1,0:T(8,128)(2,1)S(1)}, bf16[16,1536]{1,0:T(8,128)(2,1)}, u32[]{:S(2)}) copy-start(bf16[16,1536]{1,0:T(8,128)(2,1)} %param.28) | copy-start | bytes 147460
  8.4 9.4 %copy-start.9 = (bf16[16,512]{1,0:T(8,128)(2,1)S(1)}, bf16[16,512]{1,0:T(8,128)(2,1)}, u32[]{:S(2)}) copy-start(bf16[16,512]{1,0:T(8,128)(2,1)} %param.30) | copy-start | bytes 49156
  10.6 21.6 %all-to-all-start.2 = ((bf16[8,128,512]{2,1,0:T(8,128)(2,1)}), bf16[8,128,512]{2,1,0:T(8,128)(2,1)S(1)}, u32[]{:S(2)}, u32[]{:S(2)}) async-start(bf16[8,128,512]{2,1,0:T(8,128)(2,1)} %pad_maximum_fusion), calls=%async_computation.2 | async-start | bytes 2097152 | tf_op jit(solution)/shard_map/all_to_all | solution.py:709
  32.2 1.8 copy-start
  33.9 32.1 %all-to-all-start = ((bf16[8,64,2176]{2,1,0:T(8,128)(2,1)}), bf16[8,64,2176]{2,1,0:T(8,128)(2,1)S(1)}, u32[]{:S(2)}, u32[]{:S(2)}) async-start(bf16[8,64,2176]{2,1,0:T(8,128)(2,1)} %broadcast_in_dim.98), calls=%async_computation | async-start | bytes 4456448 | tf_op jit(solution)/shard_map/all_to_all | solution.py:709
  37.9 106.8 %all-gather.2.cloned.1.call-start = ((), (), s32[]{:S(2)}) async-start(), calls=%async_computation.10 | async-start | bytes 5242880 | tf_op jit(solution)/shard_map/all_gather | solution.py:715
  38.0 3.2 copy-start.5
  41.3 1.8 copy-start.10
  41.3 1.8 copy-start.11
  41.3 1.9 copy-start.16
  43.7 22.5 %copy-start.1 = (f32[8,208,8]{2,1,0:T(8,128)}, f32[8,208,8]{2,1,0:T(8,128)S(1)}, u32[]{:S(2)}) copy-start(f32[8,208,8]{2,1,0:T(8,128)S(1)} %copy.117) | copy-start | bytes 159748
  85.9 54.2 %all-to-all-start.3 = ((bf16[8,2,2,128,512]{4,3,2,1,0:T(8,128)(2,1)}), bf16[8,2,2,128,512]{4,3,2,1,0:T(8,128)(2,1)}, u32[]{:S(2)}, u32[]{:S(2)}) async-start(bf16[8,2,2,128,512]{4,3,2,1,0:T(8,128)(2,1)} %get-tuple-element.59), calls=%async_computation.3 | async-start | bytes 8388608 | tf_op jit(solution)/shard_map/all_to_all | solution.py:709
  140.1 53.7 %all-to-all-start.1 = ((bf16[8,2,2,128,512]{4,3,2,1,0:T(8,128)(2,1)}), bf16[8,2,2,128,512]{4,3,2,1,0:T(8,128)(2,1)}, u32[]{:S(2)}, u32[]{:S(2)}) async-start(bf16[8,2,2,128,512]{4,3,2,1,0:T(8,128)(2,1)} %get-tuple-element.58), calls=%async_computation.1 | async-start | bytes 8388608 | tf_op jit(solution)/shard_map/all_to_all | solution.py:709
  193.8 53.7 %all-to-all-start.5 = ((bf16[8,2,2,128,512]{4,3,2,1,0:T(8,128)(2,1)}), bf16[8,2,2,128,512]{4,3,2,1,0:T(8,128)(2,1)}, u32[]{:S(2)}, u32[]{:S(2)}) async-start(bf16[8,2,2,128,512]{4,3,2,1,0:T(8,128)(2,1)} %get-tuple-element.74), calls=%async_computation.5 | async-start | bytes 8388608 | tf_op jit(solution)/shard_map/all_to_all | solution.py:709
  198.4 151.3 %reduce-scatter.5.cloned.1.call-start = ((), (), s32[]{:S(2)}) async-start(), calls=%async_computation.12 | async-start | bytes 5242880 | tf_op jit(solution)/shard_map/reduce_scatter | solution.py:851
  219.4 28.1 %copy-start.12 = (f32[128,512]{1,0:T(8,128)}, f32[128,512]{1,0:T(8,128)S(1)}, u32[]{:S(2)}) copy-start(f32[128,512]{1,0:T(8,128)S(1)} %broadcast_dynamic-update-slice_fusion.extra_ref) | copy-start | bytes 786436
  247.5 53.7 %all-to-all-start.4 = ((bf16[8,2,2,128,512]{4,3,2,1,0:T(8,128)(2,1)}), bf16[8,2,2,128,512]{4,3,2,1,0:T(8,128)(2,1)}, u32[]{:S(2)}, u32[]{:S(2)}) async-start(bf16[8,2,2,128,512]{4,3,2,1,0:T(8,128)(2,1)} %get-tuple-element.64), calls=%async_computation.4 | async-start | bytes 8388608 | tf_op jit(solution)/shard_map/all_to_all | solution.py:709
  252.1 130.6 %reduce-scatter.3.cloned.1.call-start = ((), (), s32[]{:S(2)}) async-start(), calls=%async_computation.11 | async-start | bytes 696320 | tf_op jit(solution)/shard_map/reduce_scatter | solution.py:906
  348.5 4.8 %copy-start.23 = (f32[8]{0:T(128)S(1)}, f32[8]{0:T(128)}, u32[]{:S(2)}) copy-start(f32[8]{0:T(128)} %get-tuple-element.171) | copy-start | bytes 100
  348.5 4.8 %copy-start.3 = (bf16[8,197,512]{2,1,0:T(8,128)(2,1)S(1)}, bf16[8,197,512]{2,1,0:T(8,128)(2,1)}, u32[]{:S(2)}) copy-start(bf16[8,197,512]{2,1,0:T(8,128)(2,1)} %get-tuple-element.148) | copy-start | bytes 4841476
  349.7 35.3 %all-to-all-start.7 = ((bf16[8,128,512]{2,1,0:T(8,128)(2,1)}), bf16[8,128,512]{2,1,0:T(8,128)(2,1)S(1)}, u32[]{:S(2)}, u32[]{:S(2)}) async-start(bf16[8,128,512]{2,1,0:T(8,128)(2,1)} %reduce-scatter.5.cloned.1.call-done), calls=%async_computation.9 | async-start | bytes 2097152 | tf_op jit(solution)/shard_map/all_to_all | solution.py:709
  353.3 1.8 copy-start.4
  (2 other events, 2.1 us)
Sparse Core Ops, SparseCore 0:
  44.9 82.7 all-gather.1
  219.4 87.5 reduce-scatter.4
  349.8 32.9 reduce-scatter.2
